TPU v7x, 32 devices: a whole 2x2x4 slice. The times are simulated.
32 devices in a mesh: dp: 4 (over y, x), tensor: 8 (over z, core).
Axes of the slice: x: 2, y: 2, z: 4, core: 2. Of those that a mesh axis runs over, the one named last changes fastest.
Arguments:
- inputs: bfloat16 [4, 2048, 2048], P('dp'), may hold values from -6 to 6
- segment_ids: int32 [4, 2048], P('dp'), may hold values from 0 to 7, never falling along the last dimension, each value on 1 to 1024 neighbouring positions
- norm_gain: bfloat16 [2048], replicated, may hold values from 0.5 to 1.5
- norm_bias: bfloat16 [2048], replicated, may hold values from -2 to 2
- qkv_weight: bfloat16 [2048, 3, 2048], P(None, None, 'tensor'), may hold values from -0.125 to 0.125
- qkv_bias: bfloat16 [3, 2048], P(None, 'tensor'), may hold values from -2 to 2
- out_weight: bfloat16 [2048, 2048], P('tensor'), may hold values from -0.5 to 0.5
- out_bias: bfloat16 [2048], replicated, may hold values from -2 to 2
- up_weight: bfloat16 [2048, 8192], P(None, 'tensor'), may hold values from -0.125 to 0.125
- up_bias: bfloat16 [8192], P('tensor'), may hold values from -2 to 2
- down_weight: bfloat16 [8192, 2048], P('tensor'), may hold values from -0.0625 to 0.0625
- down_bias: bfloat16 [2048], replicated, may hold values from -2 to 2
- cotangent: bfloat16 [4, 2048, 2048], P('dp'), may hold values from -6 to 6
Outputs:
- output: bfloat16 [4, 2048, 2048], P('dp')
- input_grad: bfloat16 [4, 2048, 2048], P('dp')
- norm_gain_grad: float32 [2048], P('dp')
- norm_bias_grad: float32 [2048], P('dp')
- qkv_weight_grad: float32 [2048, 3, 2048], P('dp', None, 'tensor')
- qkv_bias_grad: float32 [3, 32, 64], P(None, 'tensor', 'dp')
- out_weight_grad: float32 [2048, 2048], P('tensor', 'dp')
- out_bias_grad: float32 [2048], P('dp')
- up_weight_grad: float32 [2048, 8192], P('dp', 'tensor')
- up_bias_grad: float32 [128, 64], P('tensor', 'dp')
- down_weight_grad: float32 [8192, 2048], P('tensor', 'dp')
- down_bias_grad: float32 [2048], P('dp')
Inputs may be any that keep to these rules, and one draw needn't show every extreme that they name: `segment_ids`: along each row the ids never fall; every document holds 1 to 1024 tokens, and one document of each row holds exactly 1024.
All inputs are finite; a program needn't handle non-finite values.
Results may differ from a plain program's by a relative error of at most 0.017.
Values may be sent and summed in bfloat16 or wider, within the bound.
A program may use at most 256 MiB of HBM per device.

v0:
```python
from functools import partial

import jax
import jax.numpy as jnp
from jax import lax
from jax.experimental import pallas as pl
from jax.experimental.pallas import tpu as pltpu
from jax.sharding import PartitionSpec as P

HD = 64
ROT = 32
PAIR = 2 * HD
TILE = 256
CHUNKS = 4
NEG = -1e30
MIB = 1 << 20
F32 = jnp.float32
BF16 = jnp.bfloat16


class Chain:
    def __init__(self):
        self.link = jnp.zeros((8, 128), F32)

    def __call__(
        self, kernel, name, grid, ins, outs, scalars=(), scratch=(), alias=(), mib=58, flops=1, collective=None
    ):
        taken, given = len(scalars) + len(ins), len(outs)

        def body(*refs):
            kernel(*refs[:taken], *refs[taken + 1 : taken + 1 + given], *refs[taken + 2 + given :])

        anywhere = pl.BlockSpec(memory_space=pltpu.HBM)
        results = pl.pallas_call(
            body,
            grid_spec=pltpu.PrefetchScalarGridSpec(
                num_scalar_prefetch=len(scalars),
                grid=(grid,),
                in_specs=[spec for _, spec in ins] + [anywhere],
                out_specs=[spec for _, _, spec in outs] + [anywhere],
                scratch_shapes=list(scratch),
            ),
            out_shape=[jax.ShapeDtypeStruct(shape, dtype) for shape, dtype, _ in outs]
            + [jax.ShapeDtypeStruct(self.link.shape, F32)],
            input_output_aliases={taken: given, **{len(scalars) + i: o for i, o in alias}},
            compiler_params=pltpu.CompilerParams(
                dimension_semantics=("arbitrary",), vmem_limit_bytes=mib * MIB,
                collective_id=collective, has_side_effects=collective is not None,
            ),
            cost_estimate=pl.CostEstimate(flops=int(flops), bytes_accessed=1, transcendentals=0),
            name=name,
        )(*scalars, *[array for array, _ in ins], self.link)
        self.link = results[-1]
        return results[:-1]


def whole(shape):
    zeros = (0,) * len(shape)
    return pl.BlockSpec(shape, lambda *i: zeros)


def rows(n, height=TILE):
    return pl.BlockSpec((height, n), lambda i, *s: (i, 0))


def nn(a, b):
    return lax.dot_general(a, b, (((1,), (0,)), ((), ())), preferred_element_type=F32)


def nt(a, b):
    return lax.dot_general(a, b, (((1,), (1,)), ((), ())), preferred_element_type=F32)


def tn(a, b):
    return lax.dot_general(a, b, (((0,), (0,)), ((), ())), preferred_element_type=F32)


def rotated(x, cos_wide, sin_wide):
    lane = lax.broadcasted_iota(jnp.int32, x.shape, 1) % HD
    half = ROT // 2
    other = jnp.where(
        lane < half, pltpu.roll(x, PAIR - half, 1), pltpu.roll(x, half, 1)
    )
    return x * cos_wide + other * sin_wide


def row_stats(x):
    mean = jnp.mean(x, axis=-1, keepdims=True)
    centered = x - mean
    inverse = lax.rsqrt(jnp.mean(centered * centered, axis=-1, keepdims=True) + 1e-05)
    return centered * inverse, mean, inverse


def gelu_both(u):
    c = 0.7978845608028654
    u2 = u * u
    gate = 0.5 + 0.5 * jnp.tanh(u * (c + (c * 0.044715) * u2))
    value = u * gate
    slope = gate + value * (1.0 - gate) * (2.0 * c + (6.0 * c * 0.044715) * u2)
    return value, slope


def first_kernel(
    x0_ref, x1_ref, x2_ref, small_ref, wq_ref, bq_ref, wu_ref, bu_ref, start_ref, freq_ref,
    normed_ref, stats_ref, q_ref, k_ref, v_ref, hidden_ref, slope_ref, cos_ref, sin_ref,
    even, odd, even_stats,
):
    s = pl.program_id(0)
    gain, shift = small_ref[0:1], small_ref[1:2]
    lane = lax.broadcasted_iota(jnp.int32, (TILE, PAIR), 1)

    def norm(x):
        scaled, mean, inverse = row_stats(x.astype(F32))
        return (scaled * gain + shift).astype(BF16), jnp.where(lane == 0, mean, inverse)

    @pl.when(s == 0)
    def _():
        even[...], even_stats[...] = norm(x0_ref[...])

    half = ROT // 2
    unit = lax.broadcasted_iota(jnp.int32, (half, PAIR), 1) % HD
    index = lax.broadcasted_iota(jnp.int32, (half, PAIR), 0)
    first_half = (unit == index).astype(F32)
    second_half = (unit == index + half).astype(F32)
    bias = bq_ref[...].astype(F32)

    def spread(a, b):
        return lax.dot_general(
            a, b, (((0,), (0,)), ((), ())), precision=lax.Precision.HIGHEST,
            preferred_element_type=F32,
        )

    def project(t, normed):
        here = slice(t * TILE, (t + 1) * TILE)
        place = lax.broadcasted_iota(jnp.int32, (1, TILE), 1) + (2 * s + t) * TILE
        angle = freq_ref[...] * (place - start_ref[:, here]).astype(F32)
        cos_wide = spread(jnp.cos(angle), first_half + second_half)
        cos_wide = jnp.where(lane % HD < ROT, cos_wide, 1.0)
        sin_wide = spread(jnp.sin(angle), second_half - first_half)
        cos_ref[here], sin_ref[here] = cos_wide, sin_wide
        for c, out in enumerate((q_ref, k_ref, v_ref)):
            packed = nn(normed, wq_ref[c]) + bias[c : c + 1]
            if c == 2:
                out[here] = packed.astype(BF16)
            else:
                for p in range(packed.shape[1] // PAIR):
                    cut = slice(p * PAIR, (p + 1) * PAIR)
                    turned = rotated(packed[:, cut], cos_wide, sin_wide).astype(BF16)
                    out[here, cut] = turned * (HD**-0.5) if c == 0 else turned
        units = wu_ref.shape[1]
        for n in range(0, units, TILE):
            cut = slice(n, n + TILE)
            value, slope = gelu_both(nn(normed, wu_ref[:, cut]) + bu_ref[:, cut])
            hidden_ref[here, cut] = value.astype(BF16)
            slope_ref[here, cut] = slope.astype(BF16)

    normed = even[...]
    normed_ref[:TILE] = normed
    stats_ref[:TILE] = even_stats[...]
    after, after_stats = norm(x1_ref[...])
    odd[...] = after
    normed_ref[TILE:] = after
    stats_ref[TILE:] = after_stats
    project(0, normed)
    even[...], even_stats[...] = norm(x2_ref[...])
    project(1, odd[...])


def first(chain, x, small, wq, bq, wu, bu, start):
    length, d = x.shape
    width, units = wq.shape[2], wu.shape[1]
    tiles = length // TILE
    freq = 10000.0 ** (-jnp.arange(ROT // 2, dtype=F32) * 2.0 / ROT)
    at = lambda f: pl.BlockSpec((TILE, d), lambda s: (f(s), 0))
    big = lambda n: rows(n, 2 * TILE)
    return chain(
        first_kernel,
        "first",
        tiles // 2,
        [
            (x, at(lambda s: 0)),
            (x, at(lambda s: 2 * s + 1)),
            (x, at(lambda s: jnp.minimum(2 * s + 2, tiles - 1))),
            (small, whole(small.shape)), (wq, whole(wq.shape)), (bq, whole(bq.shape)),
            (wu, whole(wu.shape)), (bu[None].astype(F32), whole((1, units))),
            (start[None], pl.BlockSpec((1, 2 * TILE), lambda s: (0, s))),
            (jnp.broadcast_to(freq[:, None], (ROT // 2, TILE)), whole((ROT // 2, TILE))),
        ],
        [((length, d), BF16, big(d)), ((length, PAIR), F32, big(PAIR))]
        + [((length, n), BF16, big(n)) for n in (width, width, width, units, units)]
        + [((length, PAIR), F32, big(PAIR))] * 2,
        scratch=[pltpu.VMEM((TILE, d), BF16)] * 2 + [pltpu.VMEM((TILE, PAIR), F32)],
        mib=40,
        flops=35e9,
    )


def halves(x):
    left = lax.broadcasted_iota(jnp.int32, x.shape, 1) < HD
    zero = jnp.zeros(x.shape, x.dtype)
    return [jnp.where(left, x, zero), jnp.where(left, zero, x)]


def pair_cuts(width):
    return [slice(p, p + PAIR) for p in range(0, width, PAIR)]


def attend_kernel(start_sref, start_ref, q_ref, k_ref, v_ref, mixed_ref, log_ref):
    i = pl.program_id(0)
    cuts = pair_cuts(q_ref.shape[1])
    heads = range(2 * len(cuts))
    key_row = lax.broadcasted_iota(jnp.int32, (TILE, TILE), 0)
    query = lax.broadcasted_iota(jnp.int32, (TILE, TILE), 1) + i * TILE
    start = start_ref[...]
    queries = [q for cut in cuts for q in halves(q_ref[:, cut])]

    def step(j, carry):
        tops, totals, sums = carry
        there = pl.ds(pl.multiple_of(j * TILE, TILE), TILE)
        place = key_row + j * TILE
        allowed = (place >= start) & (place <= query)
        k = [k_ref[there, cut] for cut in cuts]
        v = [v_ref[there, cut] for cut in cuts]
        s = [nt(k[h // 2], queries[h]) for h in heads]
        s = [jnp.where(allowed, a, NEG) for a in s]
        top = [jnp.maximum(tops[h], jnp.max(s[h], axis=0, keepdims=True)) for h in heads]
        alpha = [jnp.exp(tops[h] - top[h]) for h in heads]
        w = [jnp.exp(s[h] - top[h]) for h in heads]
        totals = [totals[h] * alpha[h] + jnp.sum(w[h], axis=0, keepdims=True) for h in heads]
        w = [a.astype(BF16) for a in w]
        add = [tn(v[h // 2], w[h])[h % 2 * HD : (h % 2 + 1) * HD] for h in heads]
        sums = [sums[h] * alpha[h] + add[h] for h in heads]
        return tuple(top), tuple(totals), tuple(sums)

    empty = (
        tuple(jnp.full((1, TILE), NEG, F32) for _ in heads),
        tuple(jnp.zeros((1, TILE), F32) for _ in heads),
        tuple(jnp.zeros((HD, TILE), F32) for _ in heads),
    )
    low = start_sref[i * TILE] // TILE
    tops, totals, sums = lax.fori_loop(low, i + 1, step, empty)
    log_ref[...] = jnp.zeros_like(log_ref)
    for h in heads:
        log_ref[h : h + 1] = tops[h] + jnp.log(totals[h])
    mixed_ref[...] = jnp.concatenate([sums[h] * (1.0 / totals[h]) for h in heads]).T.astype(BF16)


def attend(chain, start, q, k, v):
    length, width = q.shape
    full = whole((length, width))
    return chain(
        attend_kernel,
        "attend",
        length // TILE,
        [
            (start[None], pl.BlockSpec((1, TILE), lambda i, *s: (0, i))),
            (q, rows(width)), (k, full), (v, full),
        ],
        [
            ((length, width), BF16, rows(width)),
            ((8, length), F32, pl.BlockSpec((8, TILE), lambda i, *s: (0, i))),
        ],
        scalars=(start,),
        mib=24,
        flops=19e9,
    )


def attend_back_kernel(
    begin, start_sref, start_ref, log_ref, delta_ref, q_ref, k_ref, v_ref, g_ref, cos_ref, sin_ref,
    totals_in, *refs,
):
    gq_ref, gk_ref, gv_ref, bias_ref, totals = refs[-5:]
    j = pl.program_id(0) + begin
    length, width = q_ref.shape
    cuts = pair_cuts(width)
    heads = range(2 * len(cuts))
    here = pl.ds(pl.multiple_of(j * TILE, TILE), TILE)

    @pl.when(pl.program_id(0) == 0)
    def _():
        totals[...] = totals_in[...] if begin else jnp.zeros_like(totals)
        bias_ref[...] = jnp.zeros_like(bias_ref)

    place = j * TILE + lax.broadcasted_iota(jnp.int32, (TILE, TILE), 0)
    query = lax.broadcasted_iota(jnp.int32, (TILE, TILE), 1)
    keys = [k_ref[here, cut] for cut in cuts]
    split = [half for k in keys for half in halves(k)]
    values = [v_ref[here, cut] for cut in cuts]

    def step(i, carry):
        gk, gv = carry
        there = pl.ds(pl.multiple_of(i * TILE, TILE), TILE)
        allowed = (place >= start_ref[:, there]) & (place <= query + i * TILE)
        qs = [half for cut in cuts for half in halves(q_ref[there, cut])]
        gs = [half for cut in cuts for half in halves(g_ref[there, cut])]
        s = [nt(keys[h // 2], qs[h]) for h in heads]
        gp = [nt(values[h // 2], gs[h]) for h in heads]
        w = [jnp.exp(jnp.where(allowed, s[h] - log_ref[h : h + 1, there], NEG)) for h in heads]
        ds = [(w[h] * (gp[h] - delta_ref[h : h + 1, there])).astype(BF16) for h in heads]
        w = [a.astype(BF16) for a in w]
        both = lambda f: tuple(f(h) + f(h + 1) for h in heads[::2])
        gv = [a + b for a, b in zip(gv, both(lambda h: nn(w[h], gs[h])))]
        gk = [a + b for a, b in zip(gk, both(lambda h: nn(ds[h], qs[h])))]
        for cut, gq in zip(cuts, both(lambda h: tn(ds[h], split[h]))):
            totals[there, cut] += gq
        return tuple(gk), tuple(gv)

    high = sum((start_sref[b * TILE] < (j + 1) * TILE).astype(jnp.int32) for b in range(length // TILE))
    empty = tuple(jnp.zeros((TILE, PAIR), F32) for _ in cuts)
    gks, gvs = lax.fori_loop(j, high, step, (empty, empty))
    cos_wide, sin_wide = cos_ref[...], -sin_ref[...]
    for cut, gk, gv in zip(cuts, gks, gvs):
        gq = rotated(totals[here, cut] * (HD**-0.5), cos_wide, sin_wide).astype(BF16)
        gk = rotated(gk, cos_wide, sin_wide).astype(BF16)
        for c, (g, out) in enumerate(((gq, gq_ref), (gk, gk_ref), (gv.astype(BF16), gv_ref))):
            out[:, cut] = g
            bias_ref[c : c + 1, cut] += jnp.sum(g.astype(F32), axis=0, keepdims=True)


def attend_back(chain, begin, end, start, log, delta, q, k, v, g, cos_wide, sin_wide, before):
    length, width = q.shape
    full = whole((length, width))
    shifted = lambda n: pl.BlockSpec((TILE, n), lambda i, *s: (i + begin, 0))
    anywhere = pl.BlockSpec(memory_space=pl.ANY)
    so_far = before[:3] if begin else []
    return chain(
        partial(attend_back_kernel, begin),
        f"attend_back_{begin}",
        end - begin,
        [
            (start[None], whole((1, length))), (log, whole((8, length))), (delta, whole((8, length))),
            (q, full), (k, full), (v, full), (g, full), (cos_wide, shifted(PAIR)), (sin_wide, shifted(PAIR)),
            (before[-1], full if begin else anywhere),
        ]
        + [(a, anywhere) for a in so_far],
        [((length, width), BF16, shifted(width))] * 3
        + [((8, width), F32, whole((8, width))), ((length, width), F32, full)],
        scalars=(start,),
        alias=tuple((10 + n, n) for n in range(len(so_far))),
        flops=31e9,
    )


def place_of(chunk, core):
    return 4 * (chunk // 2) + 2 * core + chunk % 2


def own_rows(chunks, half, skip=0):
    def spec(n):
        def index(i):
            core = lax.rem(lax.axis_index("tensor"), 2)
            steps = chunks // 2
            return (skip + 2 * lax.rem(i, steps) + jnp.where(i < steps, 1 - core, core), 0)

        return pl.BlockSpec((2 * half, n), index)

    return spec


def paired(product, chunks, ins, *refs):
    given, extra, sums, held, came, send_sem, recv_sem = (
        refs[:ins], refs[ins : len(refs) - chunks - 4], refs[-chunks - 4 : -4], *refs[-4:]
    )
    i = pl.program_id(0)
    steps = chunks // 2
    half, d = sums[0].shape
    me = lax.axis_index("tensor")
    peer = me + 1 - 2 * lax.rem(me, 2)
    barrier = pltpu.get_barrier_semaphore()

    def copy(n):
        return pltpu.make_async_remote_copy(
            src_ref=held.at[n], dst_ref=came.at[n], send_sem=send_sem.at[n], recv_sem=recv_sem.at[n],
            device_id={"tensor": peer}, device_id_type=pl.DeviceIdType.MESH,
        )

    @pl.when(i == 0)
    def _():
        pl.semaphore_signal(
            barrier, inc=1, device_id={"tensor": peer}, device_id_type=pl.DeviceIdType.MESH
        )
        for e in extra:
            e[...] = jnp.zeros_like(e)

    for cut in range(0, d, 2 * TILE):
        cut = slice(cut, cut + 2 * TILE)
        total = product(cut, given, extra).astype(BF16)
        held[pl.ds(2 * i, 2), :, cut] = total.reshape(2, half, 2 * TILE)

    @pl.when(i == 0)
    def _():
        pl.semaphore_wait(barrier, 1)

    for n in range(steps):

        @pl.when(i == n)
        def _(n=n):
            copy(2 * n).start()
            copy(2 * n + 1).start()

        @pl.when(i == steps + n)
        def _(n=n):
            for c in (2 * n, 2 * n + 1):
                copy(c).wait()
                total = held[chunks + c].astype(F32) + came[c].astype(F32)
                sums[c][...] = total.astype(BF16)


def pair_call(chain, product, name, collective, chunks, half, d, ins, extra):
    return chain(
        partial(paired, product, chunks, len(ins)),
        name,
        chunks,
        ins,
        extra + [((half, d), BF16, whole((half, d)))] * chunks,
        scratch=[pltpu.VMEM((2 * chunks, half, d), BF16), pltpu.VMEM((chunks, half, d), BF16)]
        + [pltpu.SemaphoreType.DMA((chunks,))] * 2,
        flops=13e9,
        collective=collective,
    )


def branch_kernel(mixed, hidden, wo, wd, out):
    for cut in range(0, out.shape[1], 2 * TILE):
        cut = slice(cut, cut + 2 * TILE)
        out[:, cut] = (nn(mixed[...], wo[:, cut]) + nn(hidden[...], wd[:, cut])).astype(BF16)


def branch(chain, length, mixed, hidden, wo, wd):
    d = wo.shape[1]
    big = lambda n: rows(n, 2 * TILE)
    return chain(
        branch_kernel,
        "branch",
        length // (2 * TILE),
        [
            (mixed, big(mixed.shape[1])), (hidden, big(hidden.shape[1])),
            (wo, whole(wo.shape)), (wd, whole(wd.shape)),
        ],
        [((length, d), BF16, big(d))],
        mib=30,
        flops=7e9,
    )[0]


def branch_product(cut, given, extra):
    mixed, hidden, wo, wd = given
    return nn(mixed[...], wo[:, cut]) + nn(hidden[...], wd[:, cut])


def branch_rest(chain, chunks, skip, mixed, hidden, wo, wd):
    length, d = mixed.shape[0], wo.shape[1]
    half = length // (2 * (chunks + skip))
    spec = own_rows(chunks, half, skip)
    ins = [
        (mixed, spec(mixed.shape[1])), (hidden, spec(hidden.shape[1])),
        (wo, whole(wo.shape)), (wd, whole(wd.shape)),
    ]
    return pair_call(chain, branch_product, "branch_rest", 1, chunks, half, d, ins, [])


def last_kernel(
    steps, summed, x, small, rest, grad, down_in, out_in, up_in, q_in, k_in, v_in,
    output, input_grad, down, out, up, qkv,
):
    i = pl.program_id(0)
    input_grad[...] = grad[...]
    down[...] = down_in[...].astype(F32)
    out[...] = out_in[...].astype(F32)
    up[...] = up_in[...].astype(F32).T
    for c, part in enumerate((q_in, k_in, v_in)):
        qkv[c] = part[...].astype(F32).T

    @pl.when(i < steps)
    def _():
        output[...] = output_rows(summed, x[...], None, small)

    @pl.when(i >= steps)
    def _():
        output[...] = rest[...]


def last(chain, summed, x, small, rest, grad, near, far, width, units):
    length, d = x.shape
    part = near.shape[1]
    lower = summed.shape[0]
    grid = 4
    high = length // grid
    steps = lower // high
    tall, slim, thin = units // grid, width // grid, part // grid
    block = rows(d, high)
    low = pl.BlockSpec((high, d), lambda i: (jnp.minimum(i, steps - 1), 0))
    upper = pl.BlockSpec((high, d), lambda i: (jnp.maximum(i - steps, 0), 0))
    third = lambda c: pl.BlockSpec((width, thin), lambda i: (units // width + c, i))
    return chain(
        partial(last_kernel, steps), "last", grid,
        [
            (summed, low), (x, low), (small, whole(small.shape)), (rest, upper), (grad, block),
            (near, rows(part, tall)),
            (near, pl.BlockSpec((slim, part), lambda i: (units // slim + i, 0))),
            (far, rows(part, tall)), (far, third(0)), (far, third(1)), (far, third(2)),
        ],
        [
            ((length, d), BF16, block), ((length, d), BF16, block),
            ((units, part), F32, rows(part, tall)), ((width, part), F32, rows(part, slim)),
            ((part, units), F32, pl.BlockSpec((part, tall), lambda i: (0, i))),
            ((3, part, width), F32, pl.BlockSpec((3, thin, width), lambda i: (0, i, 0))),
        ],
    )


def output_rows(a, x, b, small):
    total = a[...].astype(F32)
    if b is not None:
        total = total + b[...].astype(F32)
    return (x.astype(F32) + total + small[2:3] + small[3:4]).astype(BF16)


def close_kernel(summed, x, small, grad, output, input_grad):
    output[...] = output_rows(summed, x[...], None, small)
    input_grad[...] = grad[...]


def close_both(chain, summed, x, small, grad):
    length, d = x.shape
    block = rows(d, 2 * TILE)
    return chain(
        close_kernel, "close_both", length // (2 * TILE),
        [(summed, block), (x, block), (small, whole(small.shape)), (grad, block)],
        [((length, d), BF16, block)] * 2,
    )


def back_kernel(g_ref, slope_ref, mixed_ref, wo_ref, wd_ref, pre_ref, gm_ref, delta_ref, sums_ref, up_ref):
    @pl.when(pl.program_id(0) == 0)
    def _():
        sums_ref[...] = jnp.zeros_like(sums_ref)
        up_ref[...] = jnp.zeros_like(up_ref)

    g = g_ref[...]
    for n in range(0, wd_ref.shape[0], 2 * TILE):
        cut = slice(n, n + 2 * TILE)
        pre = (nt(g, wd_ref[cut]) * slope_ref[:, cut].astype(F32)).astype(BF16)
        pre_ref[:, cut] = pre
        up_ref[0:1, cut] += jnp.sum(pre.astype(F32), axis=0, keepdims=True)
    gm = nt(g, wo_ref[...]).astype(BF16)
    gm_ref[...] = gm
    product = gm.astype(F32) * mixed_ref[...].astype(F32)
    coarse = product.astype(BF16)
    fine = (product - coarse.astype(F32)).astype(BF16)
    width = gm.shape[1]
    pick = (
        lax.broadcasted_iota(jnp.int32, (8, width), 1) // HD
        == lax.broadcasted_iota(jnp.int32, (8, width), 0)
    ).astype(BF16)
    delta_ref[...] = nt(pick, coarse) + nt(pick, fine)
    sums_ref[0:1] += jnp.sum(g.astype(F32), axis=0, keepdims=True)


def back(chain, g, slope, mixed, wo, wd):
    length, d = g.shape
    width, units = wo.shape[0], wd.shape[0]
    big = lambda n: rows(n, 2 * TILE)
    return chain(
        back_kernel,
        "back",
        length // (2 * TILE),
        [
            (g, big(d)), (slope, big(units)), (mixed, big(width)),
            (wo, whole(wo.shape)), (wd, whole(wd.shape)),
        ],
        [
            ((length, units), BF16, big(units)), ((length, width), BF16, big(width)),
            ((8, length), F32, pl.BlockSpec((8, 2 * TILE), lambda i, *s: (0, i))),
            ((8, d), F32, whole((8, d))), ((8, units), F32, whole((8, units))),
        ],
        flops=15e9,
    )


def normed_back_product(cut, given, extra):
    gq, gk, gv, pre, x, stats, wq, wu = given
    (sums,) = extra
    total = nt(pre[...], wu[cut])
    for c, g in enumerate((gq, gk, gv)):
        total = total + nt(g[...], wq[c, cut])
    scaled = (x[:, cut].astype(F32) - stats[:, 0:1]) * stats[:, 1:2]
    sums[0:1, cut] += jnp.sum(total * scaled, axis=0, keepdims=True)
    sums[1:2, cut] += jnp.sum(total, axis=0, keepdims=True)
    return total


def normed_back(chain, chunks, gq, gk, gv, pre, x, stats, wq, wu):
    length, d = x.shape
    width, units = wq.shape[2], wu.shape[1]
    half = length // (2 * chunks)
    spec = own_rows(chunks, half)
    ins = [(a, spec(width)) for a in (gq, gk, gv)] + [
        (pre, spec(units)), (x, spec(d)), (stats, spec(PAIR)),
        (wq, whole(wq.shape)), (wu, whole(wu.shape)),
    ]
    return pair_call(
        chain, normed_back_product, "normed_back", 2, chunks, half, d, ins,
        [((8, d), F32, whole((8, d)))],
    )


def weight_grad_kernel(counts, *refs):
    *lefts, right, out = refs
    i = pl.program_id(0)
    done = 0
    for left, count in zip(lefts, counts):

        @pl.when((i >= done) & (i < done + count))
        def _(left=left):
            out[...] = tn(left[...], right[...]).astype(BF16)

        done += count


def weight_grad(chain, name, lefts, right):
    length, d = right.shape
    wide = min(TILE, *[a.shape[1] for a in lefts])
    counts = tuple(a.shape[1] // wide for a in lefts)
    ins, done = [], 0
    for a, count in zip(lefts, counts):
        place = lambda i, done=done, count=count: jnp.clip(i - done, 0, count - 1)
        ins.append((a, pl.BlockSpec((length, wide), lambda i, f=place: (0, f(i)))))
        done += count
    return chain(
        partial(weight_grad_kernel, counts),
        name,
        done,
        ins + [(right, whole(right.shape))],
        [((done * wide, d), BF16, rows(d, wide))],
        flops=2 * length * d * done * wide,
    )[0]


def vectors_kernel(size, count, vectors, total, came, part, wide, sems):
    row, me = lax.axis_index("dp"), lax.axis_index("tensor")
    barrier = pltpu.get_barrier_semaphore()
    mesh = pl.DeviceIdType.MESH
    half = part.shape[0] // 2

    def by_row(n):
        peer = lax.rem(row + n, count)
        return pltpu.make_async_remote_copy(
            src_ref=vectors.at[peer], dst_ref=came.at[n], send_sem=sems.at[0, n],
            recv_sem=sems.at[1, n], device_id={"dp": peer}, device_id_type=mesh,
        )

    def by_column(n):
        peer = lax.rem(me + n, size)
        return pltpu.make_async_remote_copy(
            src_ref=part.at[pl.ds(0, half)], dst_ref=wide.at[n], send_sem=sems.at[2, n],
            recv_sem=sems.at[3, n], device_id={"tensor": peer}, device_id_type=mesh,
        )

    for n in range(1, count):
        pl.semaphore_signal(
            barrier, inc=1, device_id={"dp": lax.rem(row + n, count)}, device_id_type=mesh
        )
    for n in range(1, size):
        pl.semaphore_signal(
            barrier, inc=1, device_id={"tensor": lax.rem(me + n, size)}, device_id_type=mesh
        )
    pl.semaphore_wait(barrier, count + size - 2)
    for n in range(1, count):
        by_row(n).start()
    mine = vectors[row]
    for n in range(1, count):
        by_row(n).wait()
        mine = mine + came[n]
    part[...] = mine
    for n in range(1, size):
        by_column(n).start()
    upper = mine[:half]
    for n in range(1, size):
        by_column(n).wait()
        upper = upper + wide[n]
    total[:half] = upper
    total[half:] = mine[half:]


def add_vectors(chain, vectors, size, count):
    small = vectors.shape[1:]
    return chain(
        partial(vectors_kernel, size, count), "add_vectors", 1, [(vectors, whole(vectors.shape))],
        [(small, F32, whole(small))],
        scratch=[
            pltpu.VMEM((count, *small), F32), pltpu.VMEM(small, F32),
            pltpu.VMEM((size, small[0] // 2, small[1]), F32),
            pltpu.SemaphoreType.DMA((4, max(size, count))),
        ],
        collective=6,
    )[0]


def widen_kernel(turned, share_ref, *outs):
    at = 0
    for out, turn in zip(outs, turned):
        if len(out.shape) == 3:
            for c in range(out.shape[0]):
                out[c] = share_ref[at : at + out.shape[2]].astype(F32).T
                at += out.shape[2]
        elif turn:
            out[...] = share_ref[at : at + out.shape[1]].astype(F32).T
            at += out.shape[1]
        else:
            out[...] = share_ref[at : at + out.shape[0]].astype(F32)
            at += out.shape[0]


def widen(chain, share, shapes, turned):
    return chain(
        partial(widen_kernel, turned), "widen", 1, [(share, whole(share.shape))],
        [(shape, F32, whole(shape)) for shape in shapes], mib=32,
    )


def add_kernel(a_ref, b_ref, out_ref):
    out_ref[...] = (a_ref[...].astype(F32) + b_ref[...].astype(F32)).astype(out_ref.dtype)


def plus(chain, a, b):
    block = whole(a.shape)
    return chain(
        add_kernel, "plus", 1, [(a, block), (b, block)], [(a.shape, a.dtype, block)], mib=16
    )[0]


def choose_kernel(flag_ref, a_ref, b_ref, out_ref):
    out_ref[...] = jnp.where(flag_ref[0] > 0, b_ref[...], a_ref[...])


def choose(chain, flag, a, b):
    height, d = a.shape
    block = rows(d, height // 2)
    return chain(
        choose_kernel, "choose", 2, [(a, block), (b, block)], [(a.shape, BF16, block)],
        scalars=(flag,),
    )[0]


def assemble_kernel(core_ref, a_ref, b_ref, *rest):
    rest[-1][...] = jnp.where(core_ref[0] == pl.program_id(0), a_ref[...], b_ref[...])


def assemble(chain, core, chunk, length, a, b, so_far):
    height, d = a.shape
    block = whole((height, d))
    anywhere = pl.BlockSpec(memory_space=pl.ANY)
    return chain(
        assemble_kernel, "assemble", 2,
        [(a, block), (b, block)] + ([] if so_far is None else [(so_far, anywhere)]),
        [((length, d), BF16, pl.BlockSpec((height, d), lambda i, *s: (place_of(chunk, i), 0)))],
        scalars=(core,), alias=() if so_far is None else ((2, 0),), mib=16,
    )[0]


def close_chunk_kernel(closing, core_ref, *refs):
    refs[-1][...] = closing(*refs[:-1])


def close_chunk(chain, closing, core, chunk, a, b, own, small):
    height, d = a.shape
    part = height // 2
    block = rows(d, part)

    def mine(n):
        return pl.BlockSpec((part, n), lambda i, core: (2 * place_of(chunk, core[0]) + i, 0))

    return chain(
        partial(close_chunk_kernel, closing), "close", 2,
        [(a, block), (b, block)] + [(o, mine(o.shape[1])) for o in own] + [(small, whole(small.shape))],
        [(a.shape, BF16, block)],
        scalars=(core,),
    )[0]


def swap_cores(value, size):
    return lax.ppermute(value, "tensor", [(i, i ^ 1) for i in range(size)])


def along(value, hops):
    return lax.ppermute(
        value, "tensor", [(2 * a + c, 2 * b + c) for a, b in hops for c in (0, 1)]
    )


def grad_rows(a, b, x, stats, g, small):
    u = (a[...].astype(F32) + b[...].astype(F32)) * small[0:1]
    mean, inverse = stats[:, 0:1], stats[:, 1:2]
    scaled = (x[...].astype(F32) - mean) * inverse
    back_u = inverse * (
        u
        - jnp.mean(u, axis=-1, keepdims=True)
        - scaled * jnp.mean(u * scaled, axis=-1, keepdims=True)
    )
    return (g[...].astype(F32) + back_u).astype(BF16)


SPLIT = 4
PIECE = TILE // SPLIT


def line_kernel(
    first, gq, gk, gv, pre, x_block, stats_block, wq, wu, small, extra, x_all, g_all, stats_all, *refs
):
    parts, refs = refs[: first // SPLIT], refs[first // SPLIT :]
    output, grad, vectors = refs[:3]
    held, came, own, lines, across, x_own, g_own, stats_own, sums, by_dp, mine, by_tensor = refs[3:15]
    (
        load_sem, peer_send, peer_recv, in_send, in_recv, mid_send, mid_recv, out_send, out_recv,
        fin_send, fin_recv, keep_sem,
    ) = refs[15:]
    chunks = came.shape[0]
    i = pl.program_id(0)
    steps, pieces = 2 * chunks, SPLIT * chunks
    d = came.shape[2]
    row, me = lax.axis_index("dp"), lax.axis_index("tensor")
    count, size = by_dp.shape[0], by_tensor.shape[0]
    core = lax.rem(me, 2)
    chip = me // 2
    peer = me + 1 - 2 * core
    beside = 2 * (chip + 1 - 2 * lax.rem(chip, 2)) + core
    facing = 2 * (3 - chip) + core
    middle = (chip == 1) | (chip == 2)
    end = jnp.logical_not(middle)
    mesh = pl.DeviceIdType.MESH
    barrier = pltpu.get_barrier_semaphore()

    def remote(source, target, send_sem, recv_sem, device, axis="tensor"):
        return pltpu.make_async_remote_copy(
            src_ref=source, dst_ref=target, send_sem=send_sem, recv_sem=recv_sem,
            device_id={axis: device}, device_id_type=mesh,
        )

    shift = pieces - first
    every = pieces + first

    def place(p, before=0):
        start = place_of(p // SPLIT, core) * TILE + lax.rem(p, SPLIT) * PIECE - before
        return pl.ds(pl.multiple_of(start, PIECE), PIECE)

    def peer_copy(c):
        return remote(held.at[c], came.at[c], peer_send.at[c], peer_recv.at[c], peer)

    def in_copy(p):
        return remote(own.at[p], lines.at[p], in_send.at[p], in_recv.at[p], beside)

    def mid_copy(p):
        return remote(own.at[p], across.at[p], mid_send.at[p], mid_recv.at[p], facing)

    def out_copy(p):
        return remote(lines.at[p], lines.at[p], out_send.at[p], out_recv.at[p], beside)

    def fin_copy(p, target):
        return remote(lines.at[p], target, fin_send.at[p], fin_recv.at[p], peer)

    def keep_copy(p, target):
        return pltpu.make_async_copy(lines.at[p], target, keep_sem.at[p])

    def part_copy(p):
        return pltpu.make_async_copy(
            parts[p // SPLIT].at[pl.ds(p % SPLIT * PIECE, PIECE)], own.at[p], keep_sem.at[p]
        )

    def of(p, action):
        @pl.when(p < first)
        def _():
            action(p, output.at[place(p + shift, shift * 2 * PIECE)])

        @pl.when(p >= first)
        def _():
            action(p, grad.at[place(p - first)])

    def loads(p):
        return [
            pltpu.make_async_copy(array.at[place(p)], here.at[p], load_sem.at[n, p])
            for n, (array, here) in enumerate(((x_all, x_own), (g_all, g_own), (stats_all, stats_own)))
        ]

    def dp_copy(n):
        device = lax.rem(row + n, count)
        wide = d // count
        source = sums.at[:, pl.ds(pl.multiple_of(device * wide, 128), wide)]
        return remote(source, by_dp.at[n], load_sem.at[3, n], load_sem.at[4, n], device, "dp")

    def tensor_copy(n):
        device = lax.rem(me + n, size)
        return remote(mine, by_tensor.at[n], load_sem.at[5, n], load_sem.at[6, n], device)

    def hand_over(p, target):
        fin_copy(p, target).start()
        keep_copy(p, target).start()

    def take_in(p):
        in_copy(p).wait_recv()
        own[p] = (own[p].astype(F32) + lines[p].astype(F32)).astype(BF16)
        mid_copy(p).start()

    def finish(p):
        mid_copy(p).wait_recv()

        @pl.when(p < first)
        def _():
            q = p + shift
            lines[p] = output_rows(own[p], x_own[q], across[p], small[...])

        @pl.when(p >= first)
        def _():
            q = p - first
            lines[p] = grad_rows(own[p], across[p], x_own[q], stats_own[q], g_own[q], small[...])

        out_copy(p).start()
        of(p, hand_over)

    def each(action, begin=0, stop=every):
        lax.fori_loop(begin, stop, lambda p, _: (action(p), 0)[1], 0)

    @pl.when(i == 0)
    def _():
        for n in range(1, count):
            pl.semaphore_signal(
                barrier, inc=1, device_id={"dp": lax.rem(row + n, count)}, device_id_type=mesh
            )
        for n in range(1, size):
            pl.semaphore_signal(
                barrier, inc=1, device_id={"tensor": lax.rem(me + n, size)}, device_id_type=mesh
            )
        sums[...] = extra[...]
        for p in range(first):
            part_copy(p).start()
        pl.semaphore_wait(barrier, count + size - 2)
        for p in range(first):
            part_copy(p).wait()

    @pl.when((i == 0) & end)
    def _():
        each(lambda p: in_copy(p).start(), 0, first)

    @pl.when((i == 0) & middle)
    def _():
        each(lambda p: [load.start() for load in loads(p)], 0, pieces)
        each(lambda p: [load.wait() for load in loads(p)], 0, pieces)

    ours = lax.rem(i, 2)
    half = i // 2
    to = pl.ds(first + SPLIT * half, SPLIT)
    for cut in range(0, d, 2 * TILE):
        cut = slice(cut, cut + 2 * TILE)
        total = nt(pre[...], wu[cut])
        for c, g in enumerate((gq, gk, gv)):
            total = total + nt(g[...], wq[c, cut])
        scaled = (x_block[:, cut].astype(F32) - stats_block[:, 0:1]) * stats_block[:, 1:2]
        sums[0:1, cut] += jnp.sum(total * scaled, axis=0, keepdims=True)
        sums[1:2, cut] += jnp.sum(total, axis=0, keepdims=True)
        total = total.astype(BF16)

        @pl.when(ours == 0)
        def _():
            held[half, :, cut] = total

        @pl.when(ours == 1)
        def _():
            own[to, :, cut] = total.reshape(SPLIT, PIECE, 2 * TILE)

    @pl.when(ours == 0)
    def _():
        peer_copy(half).start()

    @pl.when(ours == 1)
    def _():
        peer_copy(half).wait_recv()
        total = own[to].astype(F32) + came[half].reshape(SPLIT, PIECE, d).astype(F32)
        own[to] = total.astype(BF16)

    @pl.when((ours == 1) & end)
    def _():
        for r in range(SPLIT):
            in_copy(first + SPLIT * half + r).start()

    early = 6
    begin = steps - early

    @pl.when((i >= begin) & middle)
    def _():
        take_in(i - begin)

    @pl.when((i > begin) & middle)
    def _():
        finish(i - begin - 1)

    @pl.when(i == steps - 1)
    def _():
        for n in range(1, count):
            dp_copy(n).start()

    def both(p, _):
        take_in(p)
        finish(p - 1)
        return 0

    def pass_on(p):
        out_copy(p).wait_recv()
        of(p, hand_over)

    some = early + 2

    @pl.when((i == steps - 1) & middle)
    def _():
        lax.fori_loop(early, some, both, 0)

    @pl.when((i == steps - 1) & end)
    def _():
        each(pass_on, 0, some)

    @pl.when(i == steps - 1)
    def _():
        wide = d // count
        total = sums[:, pl.ds(pl.multiple_of(row * wide, 128), wide)]
        for n in range(1, count):
            dp_copy(n).wait()
            total = total + by_dp[n]
        mine[...] = total
        for n in range(1, size):
            tensor_copy(n).start()

    @pl.when((i == steps - 1) & middle)
    def _():
        lax.fori_loop(some, every, both, 0)
        finish(every - 1)
        each(lambda p: (mid_copy(p).wait_send(), out_copy(p).wait_send()))

    @pl.when((i == steps - 1) & end)
    def _():
        each(pass_on, some)
        each(lambda p: in_copy(p).wait_send())

    @pl.when(i == steps - 1)
    def _():
        total = mine[...]
        for n in range(1, size):
            tensor_copy(n).wait()
            total = total + by_tensor[n]
        vectors[...] = jnp.concatenate([total[:2], mine[2:]])
        for c in range(chunks):
            peer_copy(c).wait_send()
        each(lambda p: of(p, lambda *a: (fin_copy(*a).wait(), keep_copy(*a).wait())))


def line_back(chain, parts, chunks, size, count, gq, gk, gv, pre, x, stats, wq, wu, small, extra, g):
    length, d = x.shape
    width, units = wq.shape[2], wu.shape[1]
    pieces, first = SPLIT * chunks, SPLIT * len(parts)

    def block(n):
        def index(i):
            core = lax.rem(lax.axis_index("tensor"), 2)
            mine = lax.rem(i, 2)
            return (place_of(i // 2, lax.rem(core + 1 + mine, 2)), 0)

        return pl.BlockSpec((TILE, n), index)

    def once(shape):
        zeros = (0,) * len(shape)
        return pl.BlockSpec(shape, lambda *i: zeros, pipeline_mode=pl.Buffered(1))

    far = pl.BlockSpec(memory_space=pltpu.HBM)
    rows_of = lambda n: pltpu.VMEM((n, PIECE, d), BF16)
    sems = pltpu.SemaphoreType.DMA
    vector = (8, d // count)
    return chain(
        partial(line_kernel, first),
        "line_back",
        2 * chunks,
        [(a, block(width)) for a in (gq, gk, gv)]
        + [
            (pre, block(units)), (x, block(d)), (stats, block(PAIR)), (wq, once(wq.shape)),
            (wu, once(wu.shape)), (small, once(small.shape)), (extra, once(extra.shape)),
            (x, far), (g, far), (stats, far),
        ]
        + [(p, far) for p in parts],
        [
            ((first * 2 * PIECE, d), BF16, far), ((length, d), BF16, far),
            (vector, F32, whole(vector)),
        ],
        scratch=[
            pltpu.VMEM((chunks, TILE, d), BF16), pltpu.VMEM((chunks, TILE, d), BF16),
            rows_of(first + pieces), rows_of(first + pieces), rows_of(first + pieces),
            rows_of(pieces), rows_of(pieces),
            pltpu.VMEM((pieces, PIECE, PAIR), F32),
            pltpu.VMEM((8, d), F32), pltpu.VMEM((count, *vector), F32), pltpu.VMEM(vector, F32),
            pltpu.VMEM((size, *vector), F32),
            sems((7, max(pieces, size, count))), sems((chunks,)), sems((chunks,)),
        ]
        + [sems((first + pieces,))] * 9,
        collective=5,
        flops=200e9,
        mib=62,
    )


def flow(chain, size, core, chunk, total, closing, results, key, length):
    chips = size // 2
    chip = lax.axis_index("tensor") // 2
    distance = jnp.where(chip < chips // 2, chips // 2 - 1 - chip, chip - chips // 2)
    for s in range(chips // 2 - 1):
        came = along(total, [(s, s + 1), (chips - 1 - s, chips - 2 - s)])
        yield
        total = plus(chain, total, came)
    a, b = chips // 2 - 1, chips // 2
    came = along(total, [(a, b), (b, a)])
    yield
    value = closing(chunk, total, came)
    for s in range(chips // 2 - 1):
        a, b = chips // 2 - 1 - s, chips // 2 + s
        came = along(value, [(a, a - 1), (b, b + 1)])
        yield
        value = choose(chain, (distance == s + 1).astype(jnp.int32)[None], value, came)
    peer = swap_cores(value, size)
    yield
    results[key] = assemble(chain, core, chunk, length, value, peer, results.get(key))


def on_device(
    size,
    inputs,
    segment_ids,
    norm_gain,
    norm_bias,
    qkv_weight,
    qkv_bias,
    out_weight,
    out_bias,
    up_weight,
    up_bias,
    down_weight,
    down_bias,
    cotangent,
):
    x, g, segment_row = inputs[0], cotangent[0], segment_ids[0]
    length, d = x.shape
    width, units = qkv_weight.shape[2], up_weight.shape[1]
    count = lax.axis_size("dp")
    core = (lax.axis_index("tensor") % 2).astype(jnp.int32)[None]

    start = jnp.sum((segment_row[None, :] < segment_row[:, None]).astype(jnp.int32), axis=1)
    small = jnp.stack([norm_gain, norm_bias, out_bias, down_bias] + [norm_gain] * 4).astype(F32)
    wq = qkv_weight.transpose(1, 0, 2)

    chain = Chain()
    normed, stats, q, k, v, hidden, slope, cos_wide, sin_wide = first(
        chain, x, small, wq, qkv_bias, up_weight, up_bias, start
    )
    mixed, log = attend(chain, start, q, k, v)
    rest = 2 if size == 8 else 0
    lower = length - rest * (length // CHUNKS)
    weights = (mixed, hidden, out_weight, down_weight)
    summed = lax.psum(branch(chain, lower, *weights), "tensor")
    parts = branch_rest(chain, rest, CHUNKS - rest, *weights) if rest else []

    pre, gm, delta, g_sums, up_sums = back(chain, g, slope, mixed, out_weight, down_weight)
    scatter = lambda a: lax.psum_scatter(a, "dp", scatter_dimension=1, tiled=True)
    near = scatter(weight_grad(chain, "weight_grad_g", [hidden, mixed], g))
    tiles = length // TILE
    *packed, qkv_sums, _ = attend_back(
        chain, 0, tiles, start, log, delta, q, k, v, gm, cos_wide, sin_wide, [log]
    )
    far = scatter(weight_grad(chain, "weight_grad_n", [pre, *packed], normed))

    by_share = lambda a: a.reshape(-1, count, HD // count).swapaxes(0, 1).reshape(count, -1)
    part = d // count
    narrow = jnp.concatenate([by_share(up_sums[0]), by_share(qkv_sums[:3])], axis=1)
    narrow = jnp.pad(narrow, ((0, 0), (0, part - narrow.shape[1]))).reshape(1, d)
    if size == 8:
        extra = jnp.concatenate([jnp.zeros((2, d), F32), g_sums[:1], narrow, jnp.zeros((4, d), F32)])
        upper, grad, vectors = line_back(
            chain, parts, CHUNKS, size, count, *packed, pre, x, stats, wq, up_weight, small, extra, g
        )
    else:

        results = {}

        def line(parts, closing, own, key):
            finish = lambda chunk, a, b: close_chunk(chain, closing, core, chunk, a, b, own, small)
            flows = [
                flow(chain, size, core, c, parts[c], finish, results, key, length)
                for c in range(CHUNKS)
            ]
            while flows:
                flows = [f for f in flows if next(f, flows) is None]

        norm_sums, *parts = normed_back(chain, CHUNKS, *packed, pre, x, stats, wq, up_weight)
        line(parts, grad_rows, [x, stats, g], "grad")
        vectors = jnp.concatenate([norm_sums[:2], g_sums[:1], narrow]).reshape(4, count, part)
        vectors = vectors.swapaxes(0, 1).reshape(count, -1, 128)
        vectors = add_vectors(chain, vectors, size, count).reshape(4, part)
    if size == 8:
        output, input_grad, down_share, out_share, up_share, qkv_share = last(
            chain, summed, x, small, upper, grad, near, far, width, units
        )
    else:
        output, input_grad = close_both(chain, summed, x, small, results["grad"])
        shapes = [(units, part), (width, part)]
        down_share, out_share = widen(chain, near, shapes, (False, False))
        shapes = [(part, units), (3, part, width)]
        up_share, qkv_share = widen(chain, far, shapes, (True, True))
    up_b_share = vectors[3, : units // count].reshape(-1, HD // count)
    qkv_b_share = vectors[3, units // count : (units + 3 * width) // count].reshape(3, -1, HD // count)

    return (
        output[None],
        input_grad[None],
        vectors[0],
        vectors[1],
        qkv_share.transpose(1, 0, 2),
        qkv_b_share,
        out_share,
        vectors[2],
        up_share,
        up_b_share,
        down_share,
        vectors[2],
    )


def solution(mesh):
    placed = (
        P("dp", None, None),
        P("dp", None),
        P(),
        P(),
        P(None, None, "tensor"),
        P(None, "tensor"),
        P("tensor", None),
        P(),
        P(None, "tensor"),
        P("tensor"),
        P("tensor", None),
        P(),
        P("dp", None, None),
    )
    return jax.shard_map(
        partial(on_device, mesh.shape["tensor"]),
        mesh=mesh,
        in_specs=placed,
        out_specs=(
            P("dp", None, None),
            P("dp", None, None),
            P("dp"),
            P("dp"),
            P("dp", None, "tensor"),
            P(None, "tensor", "dp"),
            P("tensor", "dp"),
            P("dp"),
            P("dp", "tensor"),
            P("tensor", "dp"),
            P("tensor", "dp"),
            P("dp"),
        ),
        check_vma=False,
    )
```

profile of v0, /device:TPU:5, one launch (start us, length us, event | category | flops | bytes accessed | tf_op | source)
XLA Modules:
  0.0 380.2 jit_solution(2798985339382117352)
XLA Ops:
  8.1 2.6 convert_reduce_fusion.refs_0_
  10.6 0.7 stack.19
  11.3 0.7 stack.20
  12.0 0.7 stack.21
  12.7 0.7 stack.22
  13.6 0.7 convert_element_type.17
  14.3 1.9 copy-done.4
  16.2 0.7 copy-done.6
  16.9 29.9 %first.1 = (bf16[2048,2048]{1,0:T(8,128)(2,1)}, f32[2048,128]{1,0:T(8,128)S(1)}, bf16[2048,256]{1,0:T(8,128)(2,1)S(1)}, bf16[2048,256]{1,0:T(8,128)(2,1)S(1)}, b...) custom-call(bf16[2048,2048]{1,0:T(8,128)(2,1)} %bitcast.26, ...), custom_call_target="tpu_custom_call", output_to_operand_aliasing={{9}: (10, {})} | custom-call | flops 35000000512 | bytes 1 | tf_op jit(solution)/shard_map/first/pallas_call | solution.py:34
  46.9 14.0 %attend.1 = (bf16[2048,256]{1,0:T(8,128)(2,1)S(1)}, f32[8,2048]{1,0:T(8,128)S(1)}, f32[8,128]{1,0:T(8,128)S(1)}) custom-call(s32[2048]{0:T(1024)S(1)} %convert_reduce_fusion.refs_0_, s32[1,2048]{1,0:T(1,128)S(1)} %bitcast.24, bf16[2048,256]{1,0:T(8,128)(2,1)S(1)} %get-tuple-element.55.refs_2_.refs_4_, ...), custom_call_target="tpu_custom_call", output_to_operand_aliasing={{2}: (5, {})} | custom-call | flops 19000000512 | bytes 1 | tf_op jit(solution)/shard_map/attend/pallas_call | solution.py:34
  61.1 5.9 %branch.1 = (bf16[1024,2048]{1,0:T(8,128)(2,1)S(1)}, f32[8,128]{1,0:T(8,128)S(1)}) custom-call(bf16[2048,256]{1,0:T(8,128)(2,1)S(1)} %get-tuple-element.59.refs_0_.refs_2_.refs_1_, bf16[2048,1024]{1,0:T(8,128)(2,1)S(1)} %get-tuple-element.60.refs_1_.refs_0_, bf16[256,2048]{1,0:T(8,128)(2,1)S(1)} %copy-done.5, ...), custom_call_target="tpu_custom_call", output_to_operand_aliasing={{1}: (4, {})} | custom-call | flops 7000000000 | bytes 1 | tf_op jit(solution)/shard_map/branch/pallas_call | solution.py:34
  67.0 2.0 copy-done
  69.0 0.2 reduce-scatter.3.cloned.1.call-start
  69.2 0.3 copy-done.2
  69.6 11.7 %branch_rest.1 = (bf16[256,2048]{1,0:T(8,128)(2,1)}, bf16[256,2048]{1,0:T(8,128)(2,1)}, f32[8,128]{1,0:T(8,128)}) custom-call(bf16[2048,256]{1,0:T(8,128)(2,1)} %copy-done.9, bf16[2048,1024]{1,0:T(8,128)(2,1)} %copy-done.8, bf16[256,2048]{1,0:T(8,128)(2,1)} %refs_3_.5, bf16[1024,2048]{1,0:T(8,128)(2,1)} %refs_4_.1, ...), custom_call_target="tpu_custom_call", output_to_operand_aliasing={{2}: (4, {})} | custom-call | flops 12999999488 | bytes 1 | tf_op jit(solution)/shard_map/branch_rest/pallas_call | solution.py:34
  81.3 18.4 %back.1 = (bf16[2048,1024]{1,0:T(8,128)(2,1)}, bf16[2048,256]{1,0:T(8,128)(2,1)}, f32[8,2048]{1,0:T(8,128)}, f32[8,2048]{1,0:T(8,128)}, f32[8,1024]{1,0:T(8,128)}, /*index=5*/f32[8,128]{1,0:T(8,128)}) custom-call(bf16[2048,2048]{1,0:T(8,128)(2,1)} %bitcast.39, bf16[2048,1024]{1,0:T(8,128)(2,1)} %get-tuple-element.64.refs_1_, ...), custom_call_target="tpu_custom_call", output_to_operand_aliasing={{5}: (5, {})} | custom-call | flops 15000000512 | bytes 1 | tf_op jit(solution)/shard_map/back/pallas_call | solution.py:34
  99.7 17.2 %weight_grad_g.1 = (bf16[1280,2048]{1,0:T(8,128)(2,1)}, f32[8,128]{1,0:T(8,128)}) custom-call(bf16[2048,1024]{1,0:T(8,128)(2,1)} %copy-done.8, bf16[2048,256]{1,0:T(8,128)(2,1)} %copy-done.9, bf16[2048,2048]{1,0:T(8,128)(2,1)} %bitcast.40, f32[8,128]{1,0:T(8,128)} %get-tuple-element.71.refs_3_), custom_call_target="tpu_custom_call", output_to_operand_aliasing={{1}: (3, {})} | custom-call | flops 10737418240 | bytes 1 | tf_op jit(solution)/shard_map/weight_grad_g/pallas_call | solution.py:34
  116.9 0.3 reduce-scatter.5.cloned.1.call-start
  117.2 26.1 %attend_back_0.1 = (bf16[2048,256]{1,0:T(8,128)(2,1)}, bf16[2048,256]{1,0:T(8,128)(2,1)}, bf16[2048,256]{1,0:T(8,128)(2,1)}, f32[8,256]{1,0:T(8,128)}, f32[2048,256]{1,0:T(8,128)}, /*index=5*/f32[8,128]{1,0:T(8,128)}) custom-call(s32[2048]{0:T(1024)} %copy-done.7, s32[1,2048]{1,0:T(1,128)} %bitcast.25, ...), custom_call_target="tpu_custom_call", output_to_operand_aliasing={{5}: (11, {})} | custom-call | flops 31000000512 | bytes 1 | tf_op jit(solution)/shard_map/attend_back_0/pallas_call | solution.py:34
  143.3 23.0 %weight_grad_n.1 = (bf16[1792,2048]{1,0:T(8,128)(2,1)}, f32[8,128]{1,0:T(8,128)}) custom-call(bf16[2048,1024]{1,0:T(8,128)(2,1)} %get-tuple-element.76.refs_0_.refs_3_, bf16[2048,256]{1,0:T(8,128)(2,1)} %get-tuple-element.73.refs_1_.refs_0_, bf16[2048,256]{1,0:T(8,128)(2,1)} %get-tuple-element.74.refs_2_.refs_1_, ...), custom_call_target="tpu_custom_call", output_to_operand_aliasing={{1}: (5, {})} | custom-call | flops 15032385536 | bytes 1 | tf_op jit(solution)/shard_map/weight_grad_n/pallas_call | solution.py:34
  166.3 0.7 copy-done.18
  167.2 0.8 slice_reduce_fusion
  168.2 0.8 slice.25
  169.1 0.7 maximum_maximum_fusion.refs_9_
  169.8 179.8 %line_back.1 = (bf16[1024,2048]{1,0:T(8,128)(2,1)}, bf16[2048,2048]{1,0:T(8,128)(2,1)}, f32[8,512]{1,0:T(8,128)}, f32[8,128]{1,0:T(8,128)}) custom-call(bf16[2048,256]{1,0:T(8,128)(2,1)} %get-tuple-element.73.refs_1_.refs_0_, bf16[2048,256]{1,0:T(8,128)(2,1)} %get-tuple-element.74.refs_2_.refs_1_, ...), custom_call_target="tpu_custom_call", output_to_operand_aliasing={{3}: (15, {})} | custom-call | flops 199999995904 | bytes 1 | tf_op jit(solution)/shard_map/line_back/pallas_call | solution.py:34
  349.7 0.7 slice_reduce_fusion.1
  350.4 0.7 reshape_squeeze.11
  351.1 1.4 fusion.1
  352.5 0.7 slice_reduce_fusion.2
  353.2 0.7 reshape_squeeze.10
  353.9 18.3 %last.1 = (bf16[2048,2048]{1,0:T(8,128)(2,1)}, bf16[2048,2048]{1,0:T(8,128)(2,1)}, f32[1024,512]{1,0:T(8,128)}, f32[256,512]{1,0:T(8,128)}, f32[512,1024]{1,0:T(...) custom-call(bf16[1024,2048]{1,0:T(8,128)(2,1)} %all-reduce.3.cloned.1.call-done.refs_0_, ...), custom_call_target="tpu_custom_call", output_to_operand_aliasing={{6}: (11, {})} | custom-call | flops 1 | bytes 1 | tf_op jit(solution)/shard_map/last/pallas_call | solution.py:34
  372.2 0.6 copy.56
  (58 shorter events, 0.8 us)
Async XLA Ops:
  8.0 345.9 %all-reduce.3.cloned.1.call-start = ((), (), s32[]{:S(2)}) async-start(), calls=%async_computation.2 | async-start | bytes 8388608 | tf_op jit(solution)/shard_map/psum | solution.py:1163
  10.6 36.3 %copy-start.7 = (s32[2048]{0:T(1024)}, s32[2048]{0:T(1024)S(1)}, u32[]{:S(2)}) copy-start(s32[2048]{0:T(1024)S(1)} %convert_reduce_fusion.refs_0_) | copy-start | bytes 24580
  13.5 33.3 %copy-start.1 = (f32[8,2048]{1,0:T(8,128)}, f32[8,2048]{1,0:T(8,128)S(1)}, u32[]{:S(2)}) copy-start(f32[8,2048]{1,0:T(8,128)S(1)} %convert_element_type.14.refs_3_.refs_8_.refs_2_) | copy-start | bytes 196612
  14.3 1.9 copy-start.4
  16.2 0.7 copy-start.6
  46.8 14.1 %copy-start.10 = (bf16[2048,256]{1,0:T(8,128)(2,1)}, bf16[2048,256]{1,0:T(8,128)(2,1)S(1)}, u32[]{:S(2)}) copy-start(bf16[2048,256]{1,0:T(8,128)(2,1)S(1)} %get-tuple-element.55.refs_2_.refs_4_) | copy-start | bytes 3145732
  46.8 14.1 %copy-start.11 = (bf16[2048,256]{1,0:T(8,128)(2,1)}, bf16[2048,256]{1,0:T(8,128)(2,1)S(1)}, u32[]{:S(2)}) copy-start(bf16[2048,256]{1,0:T(8,128)(2,1)S(1)} %get-tuple-element.56.refs_3_.refs_5_) | copy-start | bytes 3145732
  46.9 14.1 %copy-start.12 = (bf16[2048,256]{1,0:T(8,128)(2,1)}, bf16[2048,256]{1,0:T(8,128)(2,1)S(1)}, u32[]{:S(2)}) copy-start(bf16[2048,256]{1,0:T(8,128)(2,1)S(1)} %get-tuple-element.57.refs_4_.refs_6_) | copy-start | bytes 3145732
  46.9 14.1 %copy-start.13 = (f32[2048,128]{1,0:T(8,128)}, f32[2048,128]{1,0:T(8,128)S(1)}, u32[]{:S(2)}) copy-start(f32[2048,128]{1,0:T(8,128)S(1)} %get-tuple-element.77.refs_5_.refs_12_) | copy-start | bytes 3145732
  46.9 14.1 %copy-start.14 = (f32[2048,128]{1,0:T(8,128)}, f32[2048,128]{1,0:T(8,128)S(1)}, u32[]{:S(2)}) copy-start(f32[2048,128]{1,0:T(8,128)S(1)} %get-tuple-element.69.refs_8_) | copy-start | bytes 3145732
  46.9 14.1 %copy-start.15 = (f32[2048,128]{1,0:T(8,128)}, f32[2048,128]{1,0:T(8,128)S(1)}, u32[]{:S(2)}) copy-start(f32[2048,128]{1,0:T(8,128)S(1)} %get-tuple-element.70.refs_9_) | copy-start | bytes 3145732
  46.9 14.1 %copy-start.8 = (bf16[2048,1024]{1,0:T(8,128)(2,1)}, bf16[2048,1024]{1,0:T(8,128)(2,1)S(1)}, u32[]{:S(2)}) copy-start(bf16[2048,1024]{1,0:T(8,128)(2,1)S(1)} %get-tuple-element.60.refs_1_.refs_0_) | copy-start | bytes 12582916
  46.9 14.1 %copy-start.3 = (bf16[1024,2048]{1,0:T(8,128)(2,1)S(1)}, bf16[1024,2048]{1,0:T(8,128)(2,1)}, u32[]{:S(2)}) copy-start(bf16[1024,2048]{1,0:T(8,128)(2,1)} %refs_4_.1) | copy-start | bytes 12582916
  46.9 14.1 %copy-start.5 = (bf16[256,2048]{1,0:T(8,128)(2,1)S(1)}, bf16[256,2048]{1,0:T(8,128)(2,1)}, u32[]{:S(2)}) copy-start(bf16[256,2048]{1,0:T(8,128)(2,1)} %refs_3_.5) | copy-start | bytes 3145732
  61.0 5.9 %copy-start.9 = (bf16[2048,256]{1,0:T(8,128)(2,1)}, bf16[2048,256]{1,0:T(8,128)(2,1)S(1)}, u32[]{:S(2)}) copy-start(bf16[2048,256]{1,0:T(8,128)(2,1)S(1)} %get-tuple-element.59.refs_0_.refs_2_.refs_1_) | copy-start | bytes 3145732
  61.0 5.9 %copy-start.16 = (f32[8,2048]{1,0:T(8,128)}, f32[8,2048]{1,0:T(8,128)S(1)}, u32[]{:S(2)}) copy-start(f32[8,2048]{1,0:T(8,128)S(1)} %get-tuple-element.63.refs_2_.refs_10_) | copy-start | bytes 196612
  67.0 2.0 copy-start
  69.0 0.6 copy-start.2
  69.0 284.9 %reduce-scatter.3.cloned.1.call-start = ((), (), s32[]{:S(2)}) async-start(), calls=%async_computation.3 | async-start | bytes 6553600 | tf_op jit(solution)/shard_map/reduce_scatter | solution.py:1167
  116.9 237.0 %reduce-scatter.5.cloned.1.call-start = ((), (), s32[]{:S(2)}) async-start(), calls=%async_computation.4 | async-start | bytes 9175040 | tf_op jit(solution)/shard_map/reduce_scatter | solution.py:1167
  166.3 0.7 copy-start.18
  352.5 19.7 %copy-start.17 = (f32[1,512]{1,0:T(1,128)}, f32[1,512]{1,0:T(1,128)S(1)}, u32[]{:S(2)}) copy-start(f32[1,512]{1,0:T(1,128)S(1)} %get-tuple-element.98) | copy-start | bytes 6148
Sparse Core Ops, SparseCore 0:
  69.1 101.1 all-reduce.2
Sparse Core Ops, SparseCore 1:
  117.0 65.3 reduce-scatter.2
  185.8 79.4 reduce-scatter.4
where the time goes:
time: 382 us; the launch traced here: 380 us
  Pallas kernels  344 us (90%)
  between operations  15.8 us (4%)
  local copies, waits for them, and re-layouts  15.4 us (4%)
  other arithmetic  4.01 us (1%)
    pallas_call x10, Pallas kernels, __call__(): pl.pallas_call(body, grid_spec=pltpu.PrefetchScalarGridSpec(num_scalar_pr...  344 us
  transfers between devices with their start and end apart: 3, of which 0 were waited for; matrix products, arithmetic and copies ran while one was open for 2% of the time, Pallas kernels for 73%

commit v1 on v0

--- a/solution.py
+++ b/solution.py
@@ -945,6 +945,9 @@
     @pl.when((i == 0) & middle)
     def _():
         each(lambda p: [load.start() for load in loads(p)], 0, pieces)
+
+    @pl.when((i == 1) & middle)
+    def _():
         each(lambda p: [load.wait() for load in loads(p)], 0, pieces)
 
     ours = lax.rem(i, 2)
@@ -983,7 +986,7 @@
         for r in range(SPLIT):
             in_copy(first + SPLIT * half + r).start()
 
-    early = 6
+    early = steps
     begin = steps - early
 
     @pl.when((i >= begin) & middle)
@@ -1008,7 +1011,7 @@
         out_copy(p).wait_recv()
         of(p, hand_over)
 
-    some = early + 2
+    some = early + 2 * (every - early) // 3
 
     @pl.when((i == steps - 1) & middle)
     def _():

time: 382 us -> 376 us (0.984)
  Pallas kernels: 344 us -> 337 us
    pallas_call x10, Pallas kernels: 344 us -> 337 us  [__call__(): pl.pallas_call(body, grid_spec=pltpu.PrefetchScalarGridSpec(num_scalar_pr...]
  transfers between devices with their start and end apart: 3 -> 3, of which waited for: 0 -> 0; matrix products, arithmetic and copies ran while one was open for 2% -> 2% of each run, Pallas kernels for 73% -> 72%
where the time goes in v1:
time: 376 us; the launch traced here: 373 us
  Pallas kernels  337 us (90%)
  between operations  15.8 us (4%)
  local copies, waits for them, and re-layouts  15.4 us (4%)
  other arithmetic  4.01 us (1%)
    pallas_call x10, Pallas kernels, __call__(): pl.pallas_call(body, grid_spec=pltpu.PrefetchScalarGridSpec(num_scalar_pr...  337 us
  transfers between devices with their start and end apart: 3, of which 0 were waited for; matrix products, arithmetic and copies ran while one was open for 2% of the time, Pallas kernels for 72%

profile of v1, /device:TPU:5, one launch (start us, length us, event | category | flops | bytes accessed | tf_op | source)
XLA Modules:
  0.0 373.1 jit_solution(16182691867616542231)
XLA Ops:
  8.1 2.6 convert_reduce_fusion.refs_0_
  10.6 0.7 stack.19
  11.3 0.7 stack.20
  12.0 0.7 stack.21
  12.7 0.7 stack.22
  13.6 0.7 convert_element_type.17
  14.3 1.9 copy-done.4
  16.2 0.7 copy-done.6
  16.9 29.9 %first.1 = (bf16[2048,2048]{1,0:T(8,128)(2,1)}, f32[2048,128]{1,0:T(8,128)S(1)}, bf16[2048,256]{1,0:T(8,128)(2,1)S(1)}, bf16[2048,256]{1,0:T(8,128)(2,1)S(1)}, b...) custom-call(bf16[2048,2048]{1,0:T(8,128)(2,1)} %bitcast.26, ...), custom_call_target="tpu_custom_call", output_to_operand_aliasing={{9}: (10, {})} | custom-call | flops 35000000512 | bytes 1 | tf_op jit(solution)/shard_map/first/pallas_call | solution.py:34
  46.9 14.0 %attend.1 = (bf16[2048,256]{1,0:T(8,128)(2,1)S(1)}, f32[8,2048]{1,0:T(8,128)S(1)}, f32[8,128]{1,0:T(8,128)S(1)}) custom-call(s32[2048]{0:T(1024)S(1)} %convert_reduce_fusion.refs_0_, s32[1,2048]{1,0:T(1,128)S(1)} %bitcast.24, bf16[2048,256]{1,0:T(8,128)(2,1)S(1)} %get-tuple-element.55.refs_2_.refs_4_, ...), custom_call_target="tpu_custom_call", output_to_operand_aliasing={{2}: (5, {})} | custom-call | flops 19000000512 | bytes 1 | tf_op jit(solution)/shard_map/attend/pallas_call | solution.py:34
  61.1 5.9 %branch.1 = (bf16[1024,2048]{1,0:T(8,128)(2,1)S(1)}, f32[8,128]{1,0:T(8,128)S(1)}) custom-call(bf16[2048,256]{1,0:T(8,128)(2,1)S(1)} %get-tuple-element.59.refs_0_.refs_2_.refs_1_, bf16[2048,1024]{1,0:T(8,128)(2,1)S(1)} %get-tuple-element.60.refs_1_.refs_0_, bf16[256,2048]{1,0:T(8,128)(2,1)S(1)} %copy-done.5, ...), custom_call_target="tpu_custom_call", output_to_operand_aliasing={{1}: (4, {})} | custom-call | flops 7000000000 | bytes 1 | tf_op jit(solution)/shard_map/branch/pallas_call | solution.py:34
  67.0 2.0 copy-done
  69.0 0.2 reduce-scatter.3.cloned.1.call-start
  69.2 0.3 copy-done.2
  69.6 11.7 %branch_rest.1 = (bf16[256,2048]{1,0:T(8,128)(2,1)}, bf16[256,2048]{1,0:T(8,128)(2,1)}, f32[8,128]{1,0:T(8,128)}) custom-call(bf16[2048,256]{1,0:T(8,128)(2,1)} %copy-done.9, bf16[2048,1024]{1,0:T(8,128)(2,1)} %copy-done.8, bf16[256,2048]{1,0:T(8,128)(2,1)} %refs_3_.5, bf16[1024,2048]{1,0:T(8,128)(2,1)} %refs_4_.1, ...), custom_call_target="tpu_custom_call", output_to_operand_aliasing={{2}: (4, {})} | custom-call | flops 12999999488 | bytes 1 | tf_op jit(solution)/shard_map/branch_rest/pallas_call | solution.py:34
  81.3 18.4 %back.1 = (bf16[2048,1024]{1,0:T(8,128)(2,1)}, bf16[2048,256]{1,0:T(8,128)(2,1)}, f32[8,2048]{1,0:T(8,128)}, f32[8,2048]{1,0:T(8,128)}, f32[8,1024]{1,0:T(8,128)}, /*index=5*/f32[8,128]{1,0:T(8,128)}) custom-call(bf16[2048,2048]{1,0:T(8,128)(2,1)} %bitcast.39, bf16[2048,1024]{1,0:T(8,128)(2,1)} %get-tuple-element.64.refs_1_, ...), custom_call_target="tpu_custom_call", output_to_operand_aliasing={{5}: (5, {})} | custom-call | flops 15000000512 | bytes 1 | tf_op jit(solution)/shard_map/back/pallas_call | solution.py:34
  99.7 17.2 %weight_grad_g.1 = (bf16[1280,2048]{1,0:T(8,128)(2,1)}, f32[8,128]{1,0:T(8,128)}) custom-call(bf16[2048,1024]{1,0:T(8,128)(2,1)} %copy-done.8, bf16[2048,256]{1,0:T(8,128)(2,1)} %copy-done.9, bf16[2048,2048]{1,0:T(8,128)(2,1)} %bitcast.40, f32[8,128]{1,0:T(8,128)} %get-tuple-element.71.refs_3_), custom_call_target="tpu_custom_call", output_to_operand_aliasing={{1}: (3, {})} | custom-call | flops 10737418240 | bytes 1 | tf_op jit(solution)/shard_map/weight_grad_g/pallas_call | solution.py:34
  116.9 0.3 reduce-scatter.5.cloned.1.call-start
  117.2 26.1 %attend_back_0.1 = (bf16[2048,256]{1,0:T(8,128)(2,1)}, bf16[2048,256]{1,0:T(8,128)(2,1)}, bf16[2048,256]{1,0:T(8,128)(2,1)}, f32[8,256]{1,0:T(8,128)}, f32[2048,256]{1,0:T(8,128)}, /*index=5*/f32[8,128]{1,0:T(8,128)}) custom-call(s32[2048]{0:T(1024)} %copy-done.7, s32[1,2048]{1,0:T(1,128)} %bitcast.25, ...), custom_call_target="tpu_custom_call", output_to_operand_aliasing={{5}: (11, {})} | custom-call | flops 31000000512 | bytes 1 | tf_op jit(solution)/shard_map/attend_back_0/pallas_call | solution.py:34
  143.3 23.1 %weight_grad_n.1 = (bf16[1792,2048]{1,0:T(8,128)(2,1)}, f32[8,128]{1,0:T(8,128)}) custom-call(bf16[2048,1024]{1,0:T(8,128)(2,1)} %get-tuple-element.76.refs_0_.refs_3_, bf16[2048,256]{1,0:T(8,128)(2,1)} %get-tuple-element.73.refs_1_.refs_0_, bf16[2048,256]{1,0:T(8,128)(2,1)} %get-tuple-element.74.refs_2_.refs_1_, ...), custom_call_target="tpu_custom_call", output_to_operand_aliasing={{1}: (5, {})} | custom-call | flops 15032385536 | bytes 1 | tf_op jit(solution)/shard_map/weight_grad_n/pallas_call | solution.py:34
  166.5 0.7 copy-done.18
  167.3 0.8 slice_reduce_fusion
  168.3 0.8 slice.25
  169.2 0.7 maximum_maximum_fusion.refs_9_
  169.9 172.6 %line_back.1 = (bf16[1024,2048]{1,0:T(8,128)(2,1)}, bf16[2048,2048]{1,0:T(8,128)(2,1)}, f32[8,512]{1,0:T(8,128)}, f32[8,128]{1,0:T(8,128)}) custom-call(bf16[2048,256]{1,0:T(8,128)(2,1)} %get-tuple-element.73.refs_1_.refs_0_, bf16[2048,256]{1,0:T(8,128)(2,1)} %get-tuple-element.74.refs_2_.refs_1_, ...), custom_call_target="tpu_custom_call", output_to_operand_aliasing={{3}: (15, {})} | custom-call | flops 199999995904 | bytes 1 | tf_op jit(solution)/shard_map/line_back/pallas_call | solution.py:34
  342.6 0.7 slice_reduce_fusion.1
  343.3 0.7 reshape_squeeze.11
  344.0 1.4 fusion.1
  345.4 0.7 slice_reduce_fusion.2
  346.1 0.7 reshape_squeeze.10
  346.8 18.3 %last.1 = (bf16[2048,2048]{1,0:T(8,128)(2,1)}, bf16[2048,2048]{1,0:T(8,128)(2,1)}, f32[1024,512]{1,0:T(8,128)}, f32[256,512]{1,0:T(8,128)}, f32[512,1024]{1,0:T(...) custom-call(bf16[1024,2048]{1,0:T(8,128)(2,1)} %all-reduce.3.cloned.1.call-done.refs_0_, ...), custom_call_target="tpu_custom_call", output_to_operand_aliasing={{6}: (11, {})} | custom-call | flops 1 | bytes 1 | tf_op jit(solution)/shard_map/last/pallas_call | solution.py:34
  365.1 0.6 copy.56
  (58 shorter events, 0.8 us)
Async XLA Ops:
  8.0 338.8 %all-reduce.3.cloned.1.call-start = ((), (), s32[]{:S(2)}) async-start(), calls=%async_computation.2 | async-start | bytes 8388608 | tf_op jit(solution)/shard_map/psum | solution.py:1166
  10.6 36.3 %copy-start.7 = (s32[2048]{0:T(1024)}, s32[2048]{0:T(1024)S(1)}, u32[]{:S(2)}) copy-start(s32[2048]{0:T(1024)S(1)} %convert_reduce_fusion.refs_0_) | copy-start | bytes 24580
  13.5 33.3 %copy-start.1 = (f32[8,2048]{1,0:T(8,128)}, f32[8,2048]{1,0:T(8,128)S(1)}, u32[]{:S(2)}) copy-start(f32[8,2048]{1,0:T(8,128)S(1)} %convert_element_type.14.refs_3_.refs_8_.refs_2_) | copy-start | bytes 196612
  14.3 1.9 copy-start.4
  16.2 0.7 copy-start.6
  46.8 14.1 %copy-start.10 = (bf16[2048,256]{1,0:T(8,128)(2,1)}, bf16[2048,256]{1,0:T(8,128)(2,1)S(1)}, u32[]{:S(2)}) copy-start(bf16[2048,256]{1,0:T(8,128)(2,1)S(1)} %get-tuple-element.55.refs_2_.refs_4_) | copy-start | bytes 3145732
  46.8 14.1 %copy-start.11 = (bf16[2048,256]{1,0:T(8,128)(2,1)}, bf16[2048,256]{1,0:T(8,128)(2,1)S(1)}, u32[]{:S(2)}) copy-start(bf16[2048,256]{1,0:T(8,128)(2,1)S(1)} %get-tuple-element.56.refs_3_.refs_5_) | copy-start | bytes 3145732
  46.9 14.1 %copy-start.12 = (bf16[2048,256]{1,0:T(8,128)(2,1)}, bf16[2048,256]{1,0:T(8,128)(2,1)S(1)}, u32[]{:S(2)}) copy-start(bf16[2048,256]{1,0:T(8,128)(2,1)S(1)} %get-tuple-element.57.refs_4_.refs_6_) | copy-start | bytes 3145732
  46.9 14.1 %copy-start.13 = (f32[2048,128]{1,0:T(8,128)}, f32[2048,128]{1,0:T(8,128)S(1)}, u32[]{:S(2)}) copy-start(f32[2048,128]{1,0:T(8,128)S(1)} %get-tuple-element.77.refs_5_.refs_12_) | copy-start | bytes 3145732
  46.9 14.1 %copy-start.14 = (f32[2048,128]{1,0:T(8,128)}, f32[2048,128]{1,0:T(8,128)S(1)}, u32[]{:S(2)}) copy-start(f32[2048,128]{1,0:T(8,128)S(1)} %get-tuple-element.69.refs_8_) | copy-start | bytes 3145732
  46.9 14.1 %copy-start.15 = (f32[2048,128]{1,0:T(8,128)}, f32[2048,128]{1,0:T(8,128)S(1)}, u32[]{:S(2)}) copy-start(f32[2048,128]{1,0:T(8,128)S(1)} %get-tuple-element.70.refs_9_) | copy-start | bytes 3145732
  46.9 14.1 %copy-start.8 = (bf16[2048,1024]{1,0:T(8,128)(2,1)}, bf16[2048,1024]{1,0:T(8,128)(2,1)S(1)}, u32[]{:S(2)}) copy-start(bf16[2048,1024]{1,0:T(8,128)(2,1)S(1)} %get-tuple-element.60.refs_1_.refs_0_) | copy-start | bytes 12582916
  46.9 14.1 %copy-start.3 = (bf16[1024,2048]{1,0:T(8,128)(2,1)S(1)}, bf16[1024,2048]{1,0:T(8,128)(2,1)}, u32[]{:S(2)}) copy-start(bf16[1024,2048]{1,0:T(8,128)(2,1)} %refs_4_.1) | copy-start | bytes 12582916
  46.9 14.1 %copy-start.5 = (bf16[256,2048]{1,0:T(8,128)(2,1)S(1)}, bf16[256,2048]{1,0:T(8,128)(2,1)}, u32[]{:S(2)}) copy-start(bf16[256,2048]{1,0:T(8,128)(2,1)} %refs_3_.5) | copy-start | bytes 3145732
  61.0 5.9 %copy-start.9 = (bf16[2048,256]{1,0:T(8,128)(2,1)}, bf16[2048,256]{1,0:T(8,128)(2,1)S(1)}, u32[]{:S(2)}) copy-start(bf16[2048,256]{1,0:T(8,128)(2,1)S(1)} %get-tuple-element.59.refs_0_.refs_2_.refs_1_) | copy-start | bytes 3145732
  61.0 5.9 %copy-start.16 = (f32[8,2048]{1,0:T(8,128)}, f32[8,2048]{1,0:T(8,128)S(1)}, u32[]{:S(2)}) copy-start(f32[8,2048]{1,0:T(8,128)S(1)} %get-tuple-element.63.refs_2_.refs_10_) | copy-start | bytes 196612
  67.0 2.0 copy-start
  69.0 0.6 copy-start.2
  69.0 277.8 %reduce-scatter.3.cloned.1.call-start = ((), (), s32[]{:S(2)}) async-start(), calls=%async_computation.3 | async-start | bytes 6553600 | tf_op jit(solution)/shard_map/reduce_scatter | solution.py:1170
  116.9 229.9 %reduce-scatter.5.cloned.1.call-start = ((), (), s32[]{:S(2)}) async-start(), calls=%async_computation.4 | async-start | bytes 9175040 | tf_op jit(solution)/shard_map/reduce_scatter | solution.py:1170
  166.4 0.7 copy-start.18
  345.4 19.7 %copy-start.17 = (f32[1,512]{1,0:T(1,128)}, f32[1,512]{1,0:T(1,128)S(1)}, u32[]{:S(2)}) copy-start(f32[1,512]{1,0:T(1,128)S(1)} %get-tuple-element.98) | copy-start | bytes 6148
Sparse Core Ops, SparseCore 0:
  69.1 100.4 all-reduce.2
Sparse Core Ops, SparseCore 1:
  117.0 64.6 reduce-scatter.2
  185.1 79.4 reduce-scatter.4

commit v2 on v1

--- a/solution.py
+++ b/solution.py
@@ -485,14 +485,14 @@
     length, d = x.shape
     part = near.shape[1]
     lower = summed.shape[0]
-    grid = 4
+    grid = 8
     high = length // grid
     steps = lower // high
-    tall, slim, thin = units // grid, width // grid, part // grid
+    tall, slim, thin = units // grid, width // grid, 2 * part // grid
     block = rows(d, high)
     low = pl.BlockSpec((high, d), lambda i: (jnp.minimum(i, steps - 1), 0))
     upper = pl.BlockSpec((high, d), lambda i: (jnp.maximum(i - steps, 0), 0))
-    third = lambda c: pl.BlockSpec((width, thin), lambda i: (units // width + c, i))
+    third = lambda c: pl.BlockSpec((width, thin), lambda i: (units // width + c, i // 2))
     return chain(
         partial(last_kernel, steps), "last", grid,
         [
@@ -505,7 +505,7 @@
             ((length, d), BF16, block), ((length, d), BF16, block),
             ((units, part), F32, rows(part, tall)), ((width, part), F32, rows(part, slim)),
             ((part, units), F32, pl.BlockSpec((part, tall), lambda i: (0, i))),
-            ((3, part, width), F32, pl.BlockSpec((3, thin, width), lambda i: (0, i, 0))),
+            ((3, part, width), F32, pl.BlockSpec((3, thin, width), lambda i: (0, i // 2, 0))),
         ],
     )
 

time: 376 us -> 378 us (level)
  transfers between devices with their start and end apart: 3 -> 3, of which waited for: 0 -> 0; matrix products, arithmetic and copies ran while one was open for 2% -> 2% of each run, Pallas kernels for 72% -> 71%
where the time goes in v2:
time: 378 us; the launch traced here: 376 us
  Pallas kernels  340 us (90%)
  between operations  15.8 us (4%)
  local copies, waits for them, and re-layouts  15.4 us (4%)
  other arithmetic  4.01 us (1%)
    pallas_call x10, Pallas kernels, __call__(): pl.pallas_call(body, grid_spec=pltpu.PrefetchScalarGridSpec(num_scalar_pr...  340 us
  transfers between devices with their start and end apart: 3, of which 0 were waited for; matrix products, arithmetic and copies ran while one was open for 2% of the time, Pallas kernels for 71%

profile of v2, /device:TPU:5, one launch (start us, length us, event | category | flops | bytes accessed | tf_op | source)
XLA Modules:
  0.0 376.0 jit_solution(1873561148398458016)
XLA Ops:
  8.1 2.6 convert_reduce_fusion.refs_0_
  10.6 0.7 stack.19
  11.3 0.7 stack.20
  12.0 0.7 stack.21
  12.7 0.7 stack.22
  13.6 0.7 convert_element_type.17
  14.3 1.9 copy-done.4
  16.2 0.7 copy-done.6
  16.9 29.9 %first.1 = (bf16[2048,2048]{1,0:T(8,128)(2,1)}, f32[2048,128]{1,0:T(8,128)S(1)}, bf16[2048,256]{1,0:T(8,128)(2,1)S(1)}, bf16[2048,256]{1,0:T(8,128)(2,1)S(1)}, b...) custom-call(bf16[2048,2048]{1,0:T(8,128)(2,1)} %bitcast.26, ...), custom_call_target="tpu_custom_call", output_to_operand_aliasing={{9}: (10, {})} | custom-call | flops 35000000512 | bytes 1 | tf_op jit(solution)/shard_map/first/pallas_call | solution.py:34
  46.9 17.5 %attend.1 = (bf16[2048,256]{1,0:T(8,128)(2,1)S(1)}, f32[8,2048]{1,0:T(8,128)S(1)}, f32[8,128]{1,0:T(8,128)S(1)}) custom-call(s32[2048]{0:T(1024)S(1)} %convert_reduce_fusion.refs_0_, s32[1,2048]{1,0:T(1,128)S(1)} %bitcast.24, bf16[2048,256]{1,0:T(8,128)(2,1)S(1)} %get-tuple-element.55.refs_2_.refs_4_, ...), custom_call_target="tpu_custom_call", output_to_operand_aliasing={{2}: (5, {})} | custom-call | flops 19000000512 | bytes 1 | tf_op jit(solution)/shard_map/attend/pallas_call | solution.py:34
  64.6 5.9 %branch.1 = (bf16[1024,2048]{1,0:T(8,128)(2,1)S(1)}, f32[8,128]{1,0:T(8,128)S(1)}) custom-call(bf16[2048,256]{1,0:T(8,128)(2,1)S(1)} %get-tuple-element.59.refs_0_.refs_2_.refs_1_, bf16[2048,1024]{1,0:T(8,128)(2,1)S(1)} %get-tuple-element.60.refs_1_.refs_0_, bf16[256,2048]{1,0:T(8,128)(2,1)S(1)} %copy-done.5, ...), custom_call_target="tpu_custom_call", output_to_operand_aliasing={{1}: (4, {})} | custom-call | flops 7000000000 | bytes 1 | tf_op jit(solution)/shard_map/branch/pallas_call | solution.py:34
  70.5 2.0 copy-done
  72.5 0.2 reduce-scatter.3.cloned.1.call-start
  72.7 0.3 copy-done.2
  73.0 12.0 %branch_rest.1 = (bf16[256,2048]{1,0:T(8,128)(2,1)}, bf16[256,2048]{1,0:T(8,128)(2,1)}, f32[8,128]{1,0:T(8,128)}) custom-call(bf16[2048,256]{1,0:T(8,128)(2,1)} %copy-done.9, bf16[2048,1024]{1,0:T(8,128)(2,1)} %copy-done.8, bf16[256,2048]{1,0:T(8,128)(2,1)} %refs_3_.5, bf16[1024,2048]{1,0:T(8,128)(2,1)} %refs_4_.1, ...), custom_call_target="tpu_custom_call", output_to_operand_aliasing={{2}: (4, {})} | custom-call | flops 12999999488 | bytes 1 | tf_op jit(solution)/shard_map/branch_rest/pallas_call | solution.py:34
  85.0 18.5 %back.1 = (bf16[2048,1024]{1,0:T(8,128)(2,1)}, bf16[2048,256]{1,0:T(8,128)(2,1)}, f32[8,2048]{1,0:T(8,128)}, f32[8,2048]{1,0:T(8,128)}, f32[8,1024]{1,0:T(8,128)}, /*index=5*/f32[8,128]{1,0:T(8,128)}) custom-call(bf16[2048,2048]{1,0:T(8,128)(2,1)} %bitcast.39, bf16[2048,1024]{1,0:T(8,128)(2,1)} %get-tuple-element.64.refs_1_, ...), custom_call_target="tpu_custom_call", output_to_operand_aliasing={{5}: (5, {})} | custom-call | flops 15000000512 | bytes 1 | tf_op jit(solution)/shard_map/back/pallas_call | solution.py:34
  103.5 17.2 %weight_grad_g.1 = (bf16[1280,2048]{1,0:T(8,128)(2,1)}, f32[8,128]{1,0:T(8,128)}) custom-call(bf16[2048,1024]{1,0:T(8,128)(2,1)} %copy-done.8, bf16[2048,256]{1,0:T(8,128)(2,1)} %copy-done.9, bf16[2048,2048]{1,0:T(8,128)(2,1)} %bitcast.40, f32[8,128]{1,0:T(8,128)} %get-tuple-element.71.refs_3_), custom_call_target="tpu_custom_call", output_to_operand_aliasing={{1}: (3, {})} | custom-call | flops 10737418240 | bytes 1 | tf_op jit(solution)/shard_map/weight_grad_g/pallas_call | solution.py:34
  120.7 0.3 reduce-scatter.5.cloned.1.call-start
  121.0 31.1 %attend_back_0.1 = (bf16[2048,256]{1,0:T(8,128)(2,1)}, bf16[2048,256]{1,0:T(8,128)(2,1)}, bf16[2048,256]{1,0:T(8,128)(2,1)}, f32[8,256]{1,0:T(8,128)}, f32[2048,256]{1,0:T(8,128)}, /*index=5*/f32[8,128]{1,0:T(8,128)}) custom-call(s32[2048]{0:T(1024)} %copy-done.7, s32[1,2048]{1,0:T(1,128)} %bitcast.25, ...), custom_call_target="tpu_custom_call", output_to_operand_aliasing={{5}: (11, {})} | custom-call | flops 31000000512 | bytes 1 | tf_op jit(solution)/shard_map/attend_back_0/pallas_call | solution.py:34
  152.0 22.8 %weight_grad_n.1 = (bf16[1792,2048]{1,0:T(8,128)(2,1)}, f32[8,128]{1,0:T(8,128)}) custom-call(bf16[2048,1024]{1,0:T(8,128)(2,1)} %get-tuple-element.76.refs_0_.refs_3_, bf16[2048,256]{1,0:T(8,128)(2,1)} %get-tuple-element.73.refs_1_.refs_0_, bf16[2048,256]{1,0:T(8,128)(2,1)} %get-tuple-element.74.refs_2_.refs_1_, ...), custom_call_target="tpu_custom_call", output_to_operand_aliasing={{1}: (5, {})} | custom-call | flops 15032385536 | bytes 1 | tf_op jit(solution)/shard_map/weight_grad_n/pallas_call | solution.py:34
  174.9 0.7 copy-done.18
  175.7 0.8 slice_reduce_fusion
  176.7 0.8 slice.25
  177.7 0.7 maximum_maximum_fusion.refs_9_
  178.4 166.1 %line_back.1 = (bf16[1024,2048]{1,0:T(8,128)(2,1)}, bf16[2048,2048]{1,0:T(8,128)(2,1)}, f32[8,512]{1,0:T(8,128)}, f32[8,128]{1,0:T(8,128)}) custom-call(bf16[2048,256]{1,0:T(8,128)(2,1)} %get-tuple-element.73.refs_1_.refs_0_, bf16[2048,256]{1,0:T(8,128)(2,1)} %get-tuple-element.74.refs_2_.refs_1_, ...), custom_call_target="tpu_custom_call", output_to_operand_aliasing={{3}: (15, {})} | custom-call | flops 199999995904 | bytes 1 | tf_op jit(solution)/shard_map/line_back/pallas_call | solution.py:34
  344.4 0.7 slice_reduce_fusion.1
  345.1 0.7 reshape_squeeze.11
  345.8 1.4 fusion.1
  347.2 0.7 slice_reduce_fusion.2
  348.0 0.7 reshape_squeeze.10
  348.7 19.3 %last.1 = (bf16[2048,2048]{1,0:T(8,128)(2,1)}, bf16[2048,2048]{1,0:T(8,128)(2,1)}, f32[1024,512]{1,0:T(8,128)}, f32[256,512]{1,0:T(8,128)}, f32[512,1024]{1,0:T(...) custom-call(bf16[1024,2048]{1,0:T(8,128)(2,1)} %all-reduce.3.cloned.1.call-done.refs_0_, ...), custom_call_target="tpu_custom_call", output_to_operand_aliasing={{6}: (11, {})} | custom-call | flops 1 | bytes 1 | tf_op jit(solution)/shard_map/last/pallas_call | solution.py:34
  368.0 0.6 copy.56
  (58 shorter events, 0.8 us)
Async XLA Ops:
  8.0 340.6 %all-reduce.3.cloned.1.call-start = ((), (), s32[]{:S(2)}) async-start(), calls=%async_computation.2 | async-start | bytes 8388608 | tf_op jit(solution)/shard_map/psum | solution.py:1166
  10.6 36.3 %copy-start.7 = (s32[2048]{0:T(1024)}, s32[2048]{0:T(1024)S(1)}, u32[]{:S(2)}) copy-start(s32[2048]{0:T(1024)S(1)} %convert_reduce_fusion.refs_0_) | copy-start | bytes 24580
  13.5 33.3 %copy-start.1 = (f32[8,2048]{1,0:T(8,128)}, f32[8,2048]{1,0:T(8,128)S(1)}, u32[]{:S(2)}) copy-start(f32[8,2048]{1,0:T(8,128)S(1)} %convert_element_type.14.refs_3_.refs_8_.refs_2_) | copy-start | bytes 196612
  14.3 1.9 copy-start.4
  16.2 0.7 copy-start.6
  46.8 17.6 %copy-start.10 = (bf16[2048,256]{1,0:T(8,128)(2,1)}, bf16[2048,256]{1,0:T(8,128)(2,1)S(1)}, u32[]{:S(2)}) copy-start(bf16[2048,256]{1,0:T(8,128)(2,1)S(1)} %get-tuple-element.55.refs_2_.refs_4_) | copy-start | bytes 3145732
  46.8 17.6 %copy-start.11 = (bf16[2048,256]{1,0:T(8,128)(2,1)}, bf16[2048,256]{1,0:T(8,128)(2,1)S(1)}, u32[]{:S(2)}) copy-start(bf16[2048,256]{1,0:T(8,128)(2,1)S(1)} %get-tuple-element.56.refs_3_.refs_5_) | copy-start | bytes 3145732
  46.9 17.6 %copy-start.12 = (bf16[2048,256]{1,0:T(8,128)(2,1)}, bf16[2048,256]{1,0:T(8,128)(2,1)S(1)}, u32[]{:S(2)}) copy-start(bf16[2048,256]{1,0:T(8,128)(2,1)S(1)} %get-tuple-element.57.refs_4_.refs_6_) | copy-start | bytes 3145732
  46.9 17.6 %copy-start.13 = (f32[2048,128]{1,0:T(8,128)}, f32[2048,128]{1,0:T(8,128)S(1)}, u32[]{:S(2)}) copy-start(f32[2048,128]{1,0:T(8,128)S(1)} %get-tuple-element.77.refs_5_.refs_12_) | copy-start | bytes 3145732
  46.9 17.6 %copy-start.14 = (f32[2048,128]{1,0:T(8,128)}, f32[2048,128]{1,0:T(8,128)S(1)}, u32[]{:S(2)}) copy-start(f32[2048,128]{1,0:T(8,128)S(1)} %get-tuple-element.69.refs_8_) | copy-start | bytes 3145732
  46.9 17.6 %copy-start.15 = (f32[2048,128]{1,0:T(8,128)}, f32[2048,128]{1,0:T(8,128)S(1)}, u32[]{:S(2)}) copy-start(f32[2048,128]{1,0:T(8,128)S(1)} %get-tuple-element.70.refs_9_) | copy-start | bytes 3145732
  46.9 17.6 %copy-start.8 = (bf16[2048,1024]{1,0:T(8,128)(2,1)}, bf16[2048,1024]{1,0:T(8,128)(2,1)S(1)}, u32[]{:S(2)}) copy-start(bf16[2048,1024]{1,0:T(8,128)(2,1)S(1)} %get-tuple-element.60.refs_1_.refs_0_) | copy-start | bytes 12582916
  46.9 17.6 %copy-start.3 = (bf16[1024,2048]{1,0:T(8,128)(2,1)S(1)}, bf16[1024,2048]{1,0:T(8,128)(2,1)}, u32[]{:S(2)}) copy-start(bf16[1024,2048]{1,0:T(8,128)(2,1)} %refs_4_.1) | copy-start | bytes 12582916
  46.9 17.6 %copy-start.5 = (bf16[256,2048]{1,0:T(8,128)(2,1)S(1)}, bf16[256,2048]{1,0:T(8,128)(2,1)}, u32[]{:S(2)}) copy-start(bf16[256,2048]{1,0:T(8,128)(2,1)} %refs_3_.5) | copy-start | bytes 3145732
  64.5 5.9 %copy-start.9 = (bf16[2048,256]{1,0:T(8,128)(2,1)}, bf16[2048,256]{1,0:T(8,128)(2,1)S(1)}, u32[]{:S(2)}) copy-start(bf16[2048,256]{1,0:T(8,128)(2,1)S(1)} %get-tuple-element.59.refs_0_.refs_2_.refs_1_) | copy-start | bytes 3145732
  64.5 5.9 %copy-start.16 = (f32[8,2048]{1,0:T(8,128)}, f32[8,2048]{1,0:T(8,128)S(1)}, u32[]{:S(2)}) copy-start(f32[8,2048]{1,0:T(8,128)S(1)} %get-tuple-element.63.refs_2_.refs_10_) | copy-start | bytes 196612
  70.5 2.0 copy-start
  72.5 0.6 copy-start.2
  72.5 276.2 %reduce-scatter.3.cloned.1.call-start = ((), (), s32[]{:S(2)}) async-start(), calls=%async_computation.3 | async-start | bytes 6553600 | tf_op jit(solution)/shard_map/reduce_scatter | solution.py:1170
  120.7 228.0 %reduce-scatter.5.cloned.1.call-start = ((), (), s32[]{:S(2)}) async-start(), calls=%async_computation.4 | async-start | bytes 9175040 | tf_op jit(solution)/shard_map/reduce_scatter | solution.py:1170
  174.8 0.7 copy-start.18
  347.2 20.7 %copy-start.17 = (f32[1,512]{1,0:T(1,128)}, f32[1,512]{1,0:T(1,128)S(1)}, u32[]{:S(2)}) copy-start(f32[1,512]{1,0:T(1,128)S(1)} %get-tuple-element.98) | copy-start | bytes 6148
Sparse Core Ops, SparseCore 0:
  72.6 97.6 all-reduce.2
Sparse Core Ops, SparseCore 1:
  120.8 61.5 reduce-scatter.2
  185.8 79.4 reduce-scatter.4
